TPU v7x, 512 devices: a whole 4x4x16 slice. The times are simulated.
512 devices in a mesh: dp: 64 (over y, z), tensor: 8 (over x, core).
Axes of the slice: x: 4, y: 4, z: 16, core: 2. Of those that a mesh axis runs over, the one named last changes fastest.
Arguments:
- features: bfloat16 [36864, 8192], P('dp', 'tensor'), may hold values from -6 to 6
- out_grads: bfloat16 [36864, 11264], P('dp', 'tensor'), may hold values from -0.032958984 to 0.032958984
- bases: bfloat16 [8192, 512], P('tensor'), may hold values from -0.0625 to 0.0625
- moment_one: float32 [512, 11264], P('dp', 'tensor'), may hold values from -0.12 to 0.12
- moment_two: float32 [512, 11264], P('dp', 'tensor'), may hold values from 1e-05 to 0.001
Outputs:
- weight_update: bfloat16 [8192, 11264], P('dp', 'tensor')
- new_moment_one: float32 [512, 11264], P('dp', 'tensor')
- new_moment_two: float32 [512, 11264], P('dp', 'tensor')
All inputs are finite; a program needn't handle non-finite values.
Results may differ from a plain program's by a relative error of at most 0.0076.
Values may be sent and summed in bfloat16 or wider, within the bound.
No kernel may reach another device: no remote copies, remote signals or barrier semaphores. Data moves between devices by JAX's collectives and lax.ppermute only.
A program may use at most 64 MiB of HBM per device.

v0:
```python
import jax
import jax.numpy as jnp
from jax import lax
from jax.sharding import PartitionSpec as P

STEP = 100


def from_root(value, axis, root):
    mine = lax.axis_index(axis) == root
    return lax.psum(jnp.where(mine, value, jnp.zeros_like(value)), axis)


def per_device(features, out_grads, bases, moment_one, moment_two):
    local_part = jnp.dot(features, bases, preferred_element_type=jnp.float32)
    projected_low = lax.psum(local_part, "tensor").astype(jnp.bfloat16)
    shard_rows = bases.shape[0]
    update_rows = shard_rows * lax.axis_size("tensor") // lax.axis_size("dp")
    first_row = lax.axis_index("dp") * update_rows
    owner = first_row // shard_rows
    offset = first_row % shard_rows
    piece_rows = lax.dynamic_slice_in_dim(bases, offset, update_rows, 0)
    basis_block = from_root(piece_rows, "tensor", owner)
    contract = (((0,), (0,)), ((), ()))
    partial_sum = lax.dot_general(
        projected_low, out_grads, contract, preferred_element_type=jnp.float32
    )
    reduced = lax.psum_scatter(partial_sum, "dp", scatter_dimension=0, tiled=True)
    new_moment_one = 0.9 * moment_one + 0.1 * reduced
    new_moment_two = 0.999 * moment_two + 0.001 * reduced * reduced
    first_fix = 1.0 - 0.9**STEP
    second_fix = 1.0 - 0.999**STEP
    direction = (
        new_moment_one / first_fix / (jnp.sqrt(new_moment_two / second_fix) + 1e-08)
    ).astype(jnp.bfloat16)
    gathered = lax.all_gather(direction, "dp", axis=0, tiled=True)
    expanded = jnp.dot(basis_block, gathered, preferred_element_type=jnp.float32)
    return (expanded.astype(jnp.bfloat16), new_moment_one, new_moment_two)


def solution(mesh):
    return jax.shard_map(
        per_device,
        mesh=mesh,
        in_specs=(
            P("dp", "tensor"),
            P("dp", "tensor"),
            P("tensor", None),
            P("dp", "tensor"),
            P("dp", "tensor"),
        ),
        out_specs=(P("dp", "tensor"), P("dp", "tensor"), P("dp", "tensor")),
        check_vma=False,
    )
```

profile of v0, /device:TPU:4, one launch (start us, length us, event | category | flops | bytes accessed | tf_op | source)
XLA Modules:
  0.0 574.4 jit_solution(10346271176180937487)
XLA Ops:
  7.2 0.0 copy-start
  7.2 0.0 all-reduce.7.cloned.1.call-start
  7.2 2.5 fusion.4
  9.7 49.4 %all-reduce.8 = bf16[576,512]{1,0:T(8,128)(2,1)S(1)} all-reduce(f32[576,512]{1,0:T(8,128)S(1)} %fusion.4), channel_id=1, replica_groups=mesh['dp'=64,'tensor'=8] {'tensor'}, use_global_device_ids=true, to_apply=%region_1.2 | all-reduce | flops 294912 | bytes 1769472 | tf_op jit(solution)/shard_map/psum | solution.py:16
  59.1 0.0 copy-done
  59.1 3.0 fusion.5
  62.1 0.0 copy-start.1
  62.1 0.0 copy-start.2
  62.1 0.0 all-reduce.7.cloned.1.call-update
  62.1 0.0 all-reduce.5.cloned.1.call-start
  62.2 1.6 dynamic-slice_select_fusion
  63.8 0.0 all-reduce.5.cloned.1.call-update
  63.8 0.0 all-gather.2.cloned.1.call-start
  63.9 1.3 dynamic-slice
  65.8 285.0 %all-reduce.7.cloned.1.call-done = f32[512,1408]{1,0:T(8,128)} async-done(((f32[512,1408]{1,0:T(8,128)}), f32[512,1408]{1,0:T(8,128)}) %all-reduce.7.cloned.1.call-update) | async-done | bytes 2883600
  350.9 0.0 copy-done.1
  350.9 0.0 copy-done.2
  350.9 1.4 divide_convert_fusion
  352.3 0.0 all-gather.2.cloned.1.call-update
  352.3 66.9 %all-reduce.5.cloned.1.call-done = bf16[128,512]{1,0:T(8,128)(2,1)} async-done(((bf16[128,512]{1,0:T(8,128)(2,1)}), bf16[128,512]{1,0:T(8,128)(2,1)}) %all-reduce.5.cloned.1.call-update) | async-done | bytes 131088 | tf_op jit(solution)/shard_map/psum | solution.py:11
  419.2 146.1 %all-gather.2.cloned.1.call-done = bf16[512,1408]{1,0:T(8,128)(2,1)} async-done(((bf16[8,1408]{1,0:T(8,128)(2,1)}), bf16[512,1408]{1,0:T(8,128)(2,1)}) %all-gather.2.cloned.1.call-update) | async-done | bytes 1441808 | tf_op jit(solution)/shard_map/all_gather | solution.py:36
  565.3 2.6 convolution_convert_fusion
Async XLA Ops:
  7.2 51.9 %copy-start = (bf16[576,1408]{1,0:T(8,128)(2,1)S(1)}, bf16[576,1408]{1,0:T(8,128)(2,1)}, u32[]{:S(2)}) copy-start(bf16[576,1408]{1,0:T(8,128)(2,1)} %param.6) | copy-start | bytes 4866052
  7.2 343.7 %all-reduce.7.cloned.1.call-start = ((), (), s32[]{:S(2)}) async-start(), calls=%async_computation.2 | async-start | bytes 5767168
  62.1 288.7 %copy-start.1 = (f32[8,1408]{1,0:T(8,128)S(1)}, f32[8,1408]{1,0:T(8,128)}, u32[]{:S(2)}) copy-start(f32[8,1408]{1,0:T(8,128)} %param.8) | copy-start | bytes 135172
  62.1 288.7 %copy-start.2 = (f32[8,1408]{1,0:T(8,128)S(1)}, f32[8,1408]{1,0:T(8,128)}, u32[]{:S(2)}) copy-start(f32[8,1408]{1,0:T(8,128)} %param.9) | copy-start | bytes 135172
  62.1 357.1 %all-reduce.5.cloned.1.call-start = ((), (), s32[]{:S(2)}) async-start(), calls=%async_computation | async-start | bytes 262144 | tf_op jit(solution)/shard_map/psum | solution.py:11
  63.8 501.5 %all-gather.2.cloned.1.call-start = ((), (), s32[]{:S(2)}) async-start(), calls=%async_computation.1 | async-start | bytes 1464320 | tf_op jit(solution)/shard_map/all_gather | solution.py:36
Sparse Core Ops, SparseCore 0:
  62.3 288.5 all-reduce.6
  353.8 65.3 all-reduce.4
  422.2 143.1 all-gather.1
where the time goes:
time: 575 us; the launch traced here: 574 us
  waiting for transfers between devices  498 us (87%)
  blocking collectives  49.4 us (9%)
  between operations  14.5 us (3%)
  matrix products  8.04 us (1%)
    unnamed x4, waiting for transfers between devices  285 us
    all_gather x1, waiting for transfers between devices, per_device(): gathered = lax.all_gather(direction, 'dp', axis=0, tiled=True)  146 us
    psum x1, waiting for transfers between devices, from_root(): return lax.psum(jnp.where(mine, value, jnp.zeros_like(value)), axis)  66.9 us
    psum x1, blocking collectives, per_device(): projected_low = lax.psum(local_part, 'tensor').astype(jnp.bfloat16)  49.4 us
  transfers between devices with their start and end apart: 3, of which 3 were waited for; matrix products, arithmetic and copies ran while one was open for 1% of the time, Pallas kernels for 0%

commit v1 on v0

v1 whole, which is shorter than its diff:
```python
import jax
import jax.numpy as jnp
from jax import lax
from jax.sharding import Mesh, PartitionSpec as P

STEP = 100
Y, ZH, ZL, X, C = 4, 8, 2, 4, 2
BF16 = jnp.bfloat16
F32 = jnp.float32
AXES = ("y", "zh", "zl", "x", "core")
DP = ("y", "zh", "zl")
TENSOR = ("x", "core")


def exchange(blocks, axes):
    return lax.all_to_all(blocks, axes, 0, 0)


def sum_blocks(blocks):
    return jnp.sum(blocks.astype(F32), axis=0)


def project(features, bases):
    half = features.shape[0] // C
    core = lax.axis_index("core")
    halves = features.reshape(X, C, half // X, -1)
    theirs = lax.dynamic_index_in_dim(halves, 1 - core, 1, False).reshape(half, -1)
    ours = lax.dynamic_index_in_dim(halves, core, 1, False).reshape(half, -1)
    away = jnp.dot(theirs, bases, preferred_element_type=F32)
    arrived = lax.ppermute(away, "core", [(0, 1), (1, 0)])
    kept = jnp.dot(ours, bases, preferred_element_type=F32)
    kept = lax.optimization_barrier(kept)
    blocks = (kept + arrived).reshape(X, half // X, -1)
    my_tokens = sum_blocks(exchange(blocks, "x")).astype(BF16)
    return lax.all_gather(my_tokens, TENSOR, axis=0, tiled=True)


def basis_of_all_y(bases):
    rows = bases.shape[0] // 8
    z = lax.axis_index("zh") * ZL + lax.axis_index("zl")
    piece = lax.dynamic_slice_in_dim(bases, (z % 8) * rows, rows, 0)
    core, x = lax.axis_index("core"), lax.axis_index("x")
    other = lax.ppermute(piece, "core", [(0, 1), (1, 0)])
    block = jnp.where(core == z // 8, piece, other)
    blocks = [block] + [lax.ppermute(block, "x", [(i, (i + d) % X) for i in range(X)]) for d in range(1, X)]
    blocks = jnp.stack(blocks)
    blocks = jnp.concatenate([lax.dynamic_index_in_dim(blocks, (x - k) % X, 0) for k in range(X)])
    return blocks.reshape(X * rows, -1)


def per_device(features, out_grads, bases, moment_one, moment_two):
    basis_rows = basis_of_all_y(bases)
    projected_low = project(features, bases)
    partial_sum = lax.dot_general(
        projected_low, out_grads, (((0,), (0,)), ((), ())), preferred_element_type=F32
    ).astype(BF16)
    rank, columns = partial_sum.shape
    own = rank // (Y * ZH * ZL)
    blocks = partial_sum.reshape(Y, ZH, ZL, own, columns).transpose(0, 2, 1, 3, 4)
    blocks = blocks.reshape(Y * ZL, ZH * own, columns)
    near = sum_blocks(exchange(blocks, ("y", "zl"))).astype(BF16)
    reduced = sum_blocks(exchange(near.reshape(ZH, own, columns), "zh"))
    new_moment_one = 0.9 * moment_one + 0.1 * reduced
    new_moment_two = 0.999 * moment_two + 0.001 * reduced * reduced
    first_fix = 1.0 - 0.9**STEP
    second_fix = 1.0 - 0.999**STEP
    direction = (
        new_moment_one / first_fix / (jnp.sqrt(new_moment_two / second_fix) + 1e-08)
    ).astype(BF16)
    quarter = columns // Y
    quarters = direction.reshape(own, Y, quarter).transpose(1, 0, 2)
    copies = jnp.broadcast_to(quarters[:, None], (Y, ZH * ZL, own, quarter))
    copies = copies.reshape(Y * ZH * ZL, own, quarter)
    my_quarter = exchange(copies, DP).reshape(rank, quarter)
    tile = jnp.dot(basis_rows, my_quarter, preferred_element_type=F32).astype(BF16)
    tiles = exchange(tile.reshape(Y, -1, quarter), "y")
    update = tiles.transpose(1, 0, 2).reshape(-1, columns)
    return (update, new_moment_one, new_moment_two)


def solution(mesh):
    split = Mesh(mesh.devices.reshape(Y, ZH, ZL, X, C), AXES)
    cut = P(DP, TENSOR)
    return jax.shard_map(
        per_device,
        mesh=split,
        in_specs=(cut, cut, P(TENSOR, None), cut, cut),
        out_specs=(cut, cut, cut),
        check_vma=False,
    )
```

time: 575 us -> 137 us (0.24)
  the two profiles are of different devices: /device:TPU:4 before, /device:TPU:8 now
where the time goes in v1:
time: 137 us
  blocking collectives  94.7 us (69%)
  starting transfers between devices  17.9 us (13%)
  waiting for transfers between devices  13.7 us (10%)
  local copies, waits for them, and re-layouts  4.66 us (3%)
  matrix products  2.73 us (2%)
  other arithmetic  2.11 us (2%)
    all_to_all x4, blocking collectives, exchange(): return lax.all_to_all(blocks, axes, 0, 0)  81.5 us
    all_gather x1, blocking collectives, project(): return lax.all_gather(my_tokens, TENSOR, axis=0, tiled=True)  13.2 us
    ppermute x3, starting transfers between devices, basis_of_all_y(): lax.ppermute(block, 'x', [(i, (i + d) % X) for i in range(X)])  8.61 us
    ppermute x3, waiting for transfers between devices, basis_of_all_y(): lax.ppermute(block, 'x', [(i, (i + d) % X) for i in range(X)])  5.84 us
    all_to_all x1, starting transfers between devices, exchange(): return lax.all_to_all(blocks, axes, 0, 0)  5.43 us
    all_to_all x1, waiting for transfers between devices, exchange(): return lax.all_to_all(blocks, axes, 0, 0)  5.05 us
  transfers between devices with their start and end apart: 6, of which 5 were waited for; matrix products, arithmetic and copies ran while one was open for 2% of the time, Pallas kernels for 0%

profile of v1, /device:TPU:8, one launch (start us, length us, event | category | flops | bytes accessed | tf_op | source)
XLA Modules:
  0.0 136.7 jit_solution(16791458539918793103)
XLA Ops:
  0.6 0.0 copy-start
  0.6 0.0 copy-start.1
  0.7 1.5 %constant_dynamic-slice_fusion = (bf16[4,1,72,1024]{3,2,1,0:T(8,128)(2,1)S(1)}, bf16[4,1,72,1024]{3,2,1,0:T(8,128)(2,1)S(1)}) fusion(bf16[4,2,72,1024]{3,2,1,0:T(8,128)(2,1)} %bitcast.42, s32[]{:T(128)S(6)} %select_n.72, s32[]{:T(128)S(6)} %select_n.71), kind=kLoop, calls=%fused_computation.13 | loop fusion | bytes 2359304 | tf_op jit(solution)/shard_map/jit(dynamic_index_in_dim)/dynamic_slice | solution.py:27
  2.2 0.2 copy-done.1
  2.3 0.5 fusion.5
  2.8 1.9 %collective-permute-start.4 = (f32[288,512]{1,0:T(8,128)S(1)}, f32[288,512]{1,0:T(8,128)S(1)}, u32[]{:S(2)}, u32[]{:S(2)}) collective-permute-start(f32[288,512]{1,0:T(8,128)S(1)} %fusion.5), channel_id=1, source_target_pairs={{0,1},{1,0},{2,3},{3,2},{4,5},{5,4},{6,7},{7,6},{8,9},{9,8},{10,11... | collective-permute-start | bytes 1769480 | tf_op jit(solution)/shard_map/ppermute | solution.py:30
  4.7 0.5 fusion.4
  5.2 1.5 %collective-permute-done.4 = f32[288,512]{1,0:T(8,128)S(1)} collective-permute-done((f32[288,512]{1,0:T(8,128)S(1)}, f32[288,512]{1,0:T(8,128)S(1)}, u32[]{:S(2)}, u32[]{:S(2)}) %collective-permute-start.4) | collective-permute-done | bytes 589856 | tf_op jit(solution)/shard_map/ppermute | solution.py:30
  6.7 0.1 add.75
  6.8 14.6 %all_to_all.25 = f32[4,72,512]{2,1,0:T(8,128)S(1)} all-to-all(f32[4,72,512]{2,1,0:T(8,128)S(1)} %bitcast.35), channel_id=1, replica_groups=mesh['y'=4,'zh'=8,'zl'=2,'x'=4,'core'=2] {'x'}, dimensions={0} | all-to-all | bytes 1179648 | tf_op jit(solution)/shard_map/all_to_all | solution.py:16
  21.4 13.2 %all_gather.3 = bf16[576,512]{1,0:T(8,128)(2,1)S(1)} all-gather(bf16[72,512]{1,0:T(8,128)(2,1)S(1)} %reduce_sum.30), channel_id=1, replica_groups=mesh['y'=4,'zh'=8,'zl'=2,'x'=4,'core'=2] {'x','core'}, dimensions={0}, use_global_device_ids=true | all-gather | bytes 663552 | tf_op jit(solution)/shard_map/all_gather | solution.py:35
  34.6 0.0 copy-done
  34.6 1.4 %convolution_convert_fusion = bf16[512,1408]{1,0:T(8,128)(2,1)S(1)} fusion(bf16[576,512]{1,0:T(8,128)(2,1)S(1)} %all_gather.3, bf16[576,1408]{1,0:T(8,128)(2,1)S(1)} %copy-done), kind=kOutput, calls=%fused_computation | convolution fusion | flops 831193088 | bytes 3653632 | tf_op jit(solution)/shard_map/dot_general | solution.py:54
  36.0 0.1 copy.14
  36.2 26.0 %all_to_all.26 = bf16[8,64,1408]{2,1,0:T(8,128)(2,1)S(1)} all-to-all(bf16[8,64,1408]{2,1,0:T(8,128)(2,1)S(1)} %bitcast.34), channel_id=1, replica_groups=mesh['y'=4,'zh'=8,'zl'=2,'x'=4,'core'=2] {'y','zl'}, dimensions={0} | all-to-all | bytes 2883584 | tf_op jit(solution)/shard_map/all_to_all | solution.py:16
  62.2 0.0 copy-start.2
  62.2 0.0 copy-start.3
  62.2 0.2 reduce_sum.31
  62.4 30.5 %all_to_all.27 = bf16[8,8,1408]{2,1,0:T(8,128)(2,1)S(1)} all-to-all(bf16[8,8,1408]{2,1,0:T(8,128)(2,1)S(1)} %bitcast.43), channel_id=1, replica_groups=mesh['y'=4,'zh'=8,'zl'=2,'x'=4,'core'=2] {'zh'}, dimensions={0} | all-to-all | bytes 360448 | tf_op jit(solution)/shard_map/all_to_all | solution.py:16
  92.9 0.0 copy-done.2
  92.9 0.0 copy-done.3
  92.9 0.7 divide_convert_fusion
  93.6 0.1 reshape.56
  93.7 0.8 broadcast_in_dim.2
  94.5 5.4 %all-to-all-start.3 = ((bf16[64,8,352]{2,1,0:T(8,128)(2,1)}), bf16[64,8,352]{2,1,0:T(8,128)(2,1)S(1)}, u32[]{:S(2)}, u32[]{:S(2)}) async-start(bf16[64,8,352]{2,1,0:T(8,128)(2,1)} %bitcast.14), calls=%async_computation.3 | async-start | bytes 786432 | tf_op jit(solution)/shard_map/all_to_all | solution.py:16
  99.9 0.9 constant_dynamic-slice_fusion.6
  100.9 1.9 %collective-permute-start = (bf16[128,512]{1,0:T(8,128)(2,1)S(1)}, bf16[128,512]{1,0:T(8,128)(2,1)S(1)}, u32[]{:S(2)}, u32[]{:S(2)}) collective-permute-start(bf16[128,512]{1,0:T(8,128)(2,1)S(1)} %constant_dynamic-slice_fusion.6), channel_id=1, source_target_pairs={{0,1},{1,0},{2,3},{3,2},{4,5},{5,4},{6,7},{7,6},{8,9},{9,8},{10,11... | collective-permute-start | bytes 393224 | tf_op jit(solution)/shard_map/ppermute | solution.py:43
  102.8 1.3 collective-permute-done
  104.1 0.9 broadcast_select_fusion
  105.0 3.1 %collective-permute-start.3 = (bf16[128,512]{1,0:T(8,128)(2,1)S(1)}, bf16[128,512]{1,0:T(8,128)(2,1)S(1)}, u32[]{:S(2)}, u32[]{:S(2)}) collective-permute-start(bf16[128,512]{1,0:T(8,128)(2,1)S(1)} %broadcast_select_fusion), channel_id=1, source_target_pairs={{0,6},{2,0},{4,2},{6,4},{1,7},{3,1},{5,3},{7,5},{8,14},{10,8},{12,... | collective-permute-start | bytes 393224 | tf_op jit(solution)/shard_map/ppermute | solution.py:45
  108.1 2.8 %collective-permute-start.2 = (bf16[128,512]{1,0:T(8,128)(2,1)S(1)}, bf16[128,512]{1,0:T(8,128)(2,1)S(1)}, u32[]{:S(2)}, u32[]{:S(2)}) collective-permute-start(bf16[128,512]{1,0:T(8,128)(2,1)S(1)} %broadcast_select_fusion), channel_id=1, source_target_pairs={{0,4},{2,6},{4,0},{6,2},{1,5},{3,7},{5,1},{7,3},{8,12},{10,14},{12... | collective-permute-start | bytes 393224 | tf_op jit(solution)/shard_map/ppermute | solution.py:45
  110.9 2.8 %collective-permute-start.1 = (bf16[128,512]{1,0:T(8,128)(2,1)S(1)}, bf16[128,512]{1,0:T(8,128)(2,1)S(1)}, u32[]{:S(2)}, u32[]{:S(2)}) collective-permute-start(bf16[128,512]{1,0:T(8,128)(2,1)S(1)} %broadcast_select_fusion), channel_id=1, source_target_pairs={{0,2},{2,4},{4,6},{6,0},{1,3},{3,5},{5,7},{7,1},{8,10},{10,12},{12... | collective-permute-start | bytes 393224 | tf_op jit(solution)/shard_map/ppermute | solution.py:45
  113.8 0.0 collective-permute-done.3
  113.8 3.1 %collective-permute-done.2 = bf16[128,512]{1,0:T(8,128)(2,1)S(1)} collective-permute-done((bf16[128,512]{1,0:T(8,128)(2,1)S(1)}, bf16[128,512]{1,0:T(8,128)(2,1)S(1)}, u32[]{:S(2)}, u32[]{:S(2)}) %collective-permute-start.2) | collective-permute-done | bytes 131104 | tf_op jit(solution)/shard_map/ppermute | solution.py:45
  116.9 2.7 %collective-permute-done.1 = bf16[128,512]{1,0:T(8,128)(2,1)S(1)} collective-permute-done((bf16[128,512]{1,0:T(8,128)(2,1)S(1)}, bf16[128,512]{1,0:T(8,128)(2,1)S(1)}, u32[]{:S(2)}, u32[]{:S(2)}) %collective-permute-start.1) | collective-permute-done | bytes 131104 | tf_op jit(solution)/shard_map/ppermute | solution.py:45
  119.6 0.1 pad_maximum_fusion
  119.7 0.1 pad_maximum_fusion.1
  119.8 5.0 %all-to-all-done.3 = bf16[64,8,352]{2,1,0:T(8,128)(2,1)S(1)} async-done(((bf16[64,8,352]{2,1,0:T(8,128)(2,1)}), bf16[64,8,352]{2,1,0:T(8,128)(2,1)S(1)}, u32[]{:S(2)}, u32[]{:S(2)}) %all-to-all-start.3) | async-done | bytes 360480 | tf_op jit(solution)/shard_map/all_to_all | solution.py:16
  124.9 0.4 fusion
  125.3 0.1 copy.20
  125.3 10.5 %all_to_all.28 = bf16[4,128,352]{1,2,0:T(8,128)(2,1)S(1)} all-to-all(bf16[4,128,352]{1,2,0:T(8,128)(2,1)S(1)} %bitcast.40), channel_id=1, replica_groups=mesh['y'=4,'zh'=8,'zl'=2,'x'=4,'core'=2] {'y'}, dimensions={0} | all-to-all | bytes 720896 | tf_op jit(solution)/shard_map/all_to_all | solution.py:16
  135.8 0.9 copy.17
  (4 shorter events, 0.1 us)
Async XLA Ops:
  0.6 34.0 %copy-start = (bf16[576,1408]{1,0:T(8,128)(2,1)S(1)}, bf16[576,1408]{1,0:T(8,128)(2,1)}, u32[]{:S(2)}) copy-start(bf16[576,1408]{1,0:T(8,128)(2,1)} %param.6) | copy-start | bytes 4866052
  0.6 1.7 %copy-start.1 = (bf16[1024,512]{1,0:T(8,128)(2,1)S(1)}, bf16[1024,512]{1,0:T(8,128)(2,1)}, u32[]{:S(2)}) copy-start(bf16[1024,512]{1,0:T(8,128)(2,1)} %param.7) | copy-start | bytes 3145732
  2.8 3.9 %collective-permute-start.4 = (f32[288,512]{1,0:T(8,128)S(1)}, f32[288,512]{1,0:T(8,128)S(1)}, u32[]{:S(2)}, u32[]{:S(2)}) collective-permute-start(f32[288,512]{1,0:T(8,128)S(1)} %fusion.5), channel_id=1, source_target_pairs={{0,1},{1,0},{2,3},{3,2},{4,5},{5,4},{6,7},{7,6},{8,9},{9,8},{10,11... | collective-permute-start | bytes 1769480 | tf_op jit(solution)/shard_map/ppermute | solution.py:30
  62.2 30.7 %copy-start.2 = (f32[8,1408]{1,0:T(8,128)S(1)}, f32[8,1408]{1,0:T(8,128)}, u32[]{:S(2)}) copy-start(f32[8,1408]{1,0:T(8,128)} %param.8) | copy-start | bytes 135172
  62.2 30.7 %copy-start.3 = (f32[8,1408]{1,0:T(8,128)S(1)}, f32[8,1408]{1,0:T(8,128)}, u32[]{:S(2)}) copy-start(f32[8,1408]{1,0:T(8,128)} %param.9) | copy-start | bytes 135172
  94.5 30.4 %all-to-all-start.3 = ((bf16[64,8,352]{2,1,0:T(8,128)(2,1)}), bf16[64,8,352]{2,1,0:T(8,128)(2,1)S(1)}, u32[]{:S(2)}, u32[]{:S(2)}) async-start(bf16[64,8,352]{2,1,0:T(8,128)(2,1)} %bitcast.14), calls=%async_computation.3 | async-start | bytes 786432 | tf_op jit(solution)/shard_map/all_to_all | solution.py:16
  100.9 3.2 %collective-permute-start = (bf16[128,512]{1,0:T(8,128)(2,1)S(1)}, bf16[128,512]{1,0:T(8,128)(2,1)S(1)}, u32[]{:S(2)}, u32[]{:S(2)}) collective-permute-start(bf16[128,512]{1,0:T(8,128)(2,1)S(1)} %constant_dynamic-slice_fusion.6), channel_id=1, source_target_pairs={{0,1},{1,0},{2,3},{3,2},{4,5},{5,4},{6,7},{7,6},{8,9},{9,8},{10,11... | collective-permute-start | bytes 393224 | tf_op jit(solution)/shard_map/ppermute | solution.py:43
  105.0 8.7 %collective-permute-start.3 = (bf16[128,512]{1,0:T(8,128)(2,1)S(1)}, bf16[128,512]{1,0:T(8,128)(2,1)S(1)}, u32[]{:S(2)}, u32[]{:S(2)}) collective-permute-start(bf16[128,512]{1,0:T(8,128)(2,1)S(1)} %broadcast_select_fusion), channel_id=1, source_target_pairs={{0,6},{2,0},{4,2},{6,4},{1,7},{3,1},{5,3},{7,5},{8,14},{10,8},{12,... | collective-permute-start | bytes 393224 | tf_op jit(solution)/shard_map/ppermute | solution.py:45
  108.1 8.7 %collective-permute-start.2 = (bf16[128,512]{1,0:T(8,128)(2,1)S(1)}, bf16[128,512]{1,0:T(8,128)(2,1)S(1)}, u32[]{:S(2)}, u32[]{:S(2)}) collective-permute-start(bf16[128,512]{1,0:T(8,128)(2,1)S(1)} %broadcast_select_fusion), channel_id=1, source_target_pairs={{0,4},{2,6},{4,0},{6,2},{1,5},{3,7},{5,1},{7,3},{8,12},{10,14},{12... | collective-permute-start | bytes 393224 | tf_op jit(solution)/shard_map/ppermute | solution.py:45
  110.9 8.7 %collective-permute-start.1 = (bf16[128,512]{1,0:T(8,128)(2,1)S(1)}, bf16[128,512]{1,0:T(8,128)(2,1)S(1)}, u32[]{:S(2)}, u32[]{:S(2)}) collective-permute-start(bf16[128,512]{1,0:T(8,128)(2,1)S(1)} %broadcast_select_fusion), channel_id=1, source_target_pairs={{0,2},{2,4},{4,6},{6,0},{1,3},{3,5},{5,7},{7,1},{8,10},{10,12},{12... | collective-permute-start | bytes 393224 | tf_op jit(solution)/shard_map/ppermute | solution.py:45

commit v2 on v1

--- a/solution.py
+++ b/solution.py
@@ -35,21 +35,25 @@
     return lax.all_gather(my_tokens, TENSOR, axis=0, tiled=True)
 
 
-def basis_of_all_y(bases):
-    rows = bases.shape[0] // 8
-    z = lax.axis_index("zh") * ZL + lax.axis_index("zl")
-    piece = lax.dynamic_slice_in_dim(bases, (z % 8) * rows, rows, 0)
-    core, x = lax.axis_index("core"), lax.axis_index("x")
+def basis_rows_of_pair(bases):
+    rows = bases.shape[0] // 8 * ZL
+    zh = lax.axis_index("zh")
+    x = lax.axis_index("x")
+    piece = lax.dynamic_slice_in_dim(bases, (zh % 4) * rows, rows, 0)
     other = lax.ppermute(piece, "core", [(0, 1), (1, 0)])
-    block = jnp.where(core == z // 8, piece, other)
-    blocks = [block] + [lax.ppermute(block, "x", [(i, (i + d) % X) for i in range(X)]) for d in range(1, X)]
-    blocks = jnp.stack(blocks)
-    blocks = jnp.concatenate([lax.dynamic_index_in_dim(blocks, (x - k) % X, 0) for k in range(X)])
-    return blocks.reshape(X * rows, -1)
+    block = jnp.where(lax.axis_index("core") == zh // 4, piece, other)
+    blocks = [block]
+    for step in range(1, X):
+        pairs = [(i, (i + step) % X) for i in range(X)]
+        blocks.append(lax.ppermute(block, "x", pairs))
+    stacked = jnp.stack(blocks)
+    return jnp.concatenate(
+        [lax.dynamic_index_in_dim(stacked, (x - i) % X, 0, False) for i in range(X)]
+    )
 
 
 def per_device(features, out_grads, bases, moment_one, moment_two):
-    basis_rows = basis_of_all_y(bases)
+    basis_rows = basis_rows_of_pair(bases)
     projected_low = project(features, bases)
     partial_sum = lax.dot_general(
         projected_low, out_grads, (((0,), (0,)), ((), ())), preferred_element_type=F32
@@ -67,13 +71,14 @@
     direction = (
         new_moment_one / first_fix / (jnp.sqrt(new_moment_two / second_fix) + 1e-08)
     ).astype(BF16)
-    quarter = columns // Y
-    quarters = direction.reshape(own, Y, quarter).transpose(1, 0, 2)
-    copies = jnp.broadcast_to(quarters[:, None], (Y, ZH * ZL, own, quarter))
-    copies = copies.reshape(Y * ZH * ZL, own, quarter)
-    my_quarter = exchange(copies, DP).reshape(rank, quarter)
-    tile = jnp.dot(basis_rows, my_quarter, preferred_element_type=F32).astype(BF16)
-    tiles = exchange(tile.reshape(Y, -1, quarter), "y")
+    parts = Y * ZL
+    width = columns // parts
+    pieces = direction.reshape(own, Y, 1, ZL, width).transpose(1, 2, 3, 0, 4)
+    copies = jnp.broadcast_to(pieces, (Y, ZH, ZL, own, width))
+    copies = copies.reshape(parts * ZH, own, width)
+    my_columns = exchange(copies, DP).reshape(rank, width)
+    tile = jnp.dot(basis_rows, my_columns, preferred_element_type=F32).astype(BF16)
+    tiles = exchange(tile.reshape(parts, -1, width), ("y", "zl"))
     update = tiles.transpose(1, 0, 2).reshape(-1, columns)
     return (update, new_moment_one, new_moment_two)
 

time: 137 us -> 136 us (level)
  the two profiles are of different devices: /device:TPU:8 before, /device:TPU:64 now
where the time goes in v2:
time: 136 us; the launch traced here: 135 us
  blocking collectives  67 us (49%)
  starting transfers between devices  32.1 us (24%)
  waiting for transfers between devices  25.2 us (19%)
  local copies, waits for them, and re-layouts  3.74 us (3%)
  other arithmetic  3.33 us (2%)
  matrix products  2.83 us (2%)
    all_to_all x3, blocking collectives, exchange(): return lax.all_to_all(blocks, axes, 0, 0)  53.8 us
    all_to_all x2, starting transfers between devices, exchange(): return lax.all_to_all(blocks, axes, 0, 0)  19.7 us
    all_to_all x2, waiting for transfers between devices, exchange(): return lax.all_to_all(blocks, axes, 0, 0)  13.4 us
    all_gather x1, blocking collectives, project(): return lax.all_gather(my_tokens, TENSOR, axis=0, tiled=True)  13.2 us
    ppermute x3, waiting for transfers between devices, basis_rows_of_pair(): blocks.append(lax.ppermute(block, 'x', pairs))  10.3 us
    ppermute x3, starting transfers between devices, basis_rows_of_pair(): blocks.append(lax.ppermute(block, 'x', pairs))  8.61 us
  transfers between devices with their start and end apart: 7, of which 5 were waited for; matrix products, arithmetic and copies ran while one was open for 2% of the time, Pallas kernels for 0%

profile of v2, /device:TPU:64, one launch (start us, length us, event | category | flops | bytes accessed | tf_op | source)
XLA Modules:
  0.0 135.2 jit_solution(16043325488350592170)
XLA Ops:
  0.6 0.0 copy-start
  0.6 0.0 copy-start.1
  0.7 1.5 %constant_dynamic-slice_fusion = (bf16[4,1,72,1024]{3,2,1,0:T(8,128)(2,1)S(1)}, bf16[4,1,72,1024]{3,2,1,0:T(8,128)(2,1)S(1)}) fusion(bf16[4,2,72,1024]{3,2,1,0:T(8,128)(2,1)} %bitcast.49, s32[]{:T(128)S(6)} %select_n.72, s32[]{:T(128)S(6)} %select_n.71), kind=kLoop, calls=%fused_computation.23 | loop fusion | bytes 2359304 | tf_op jit(solution)/shard_map/jit(dynamic_index_in_dim)/dynamic_slice | solution.py:27
  2.2 0.2 copy-done.1
  2.3 0.5 fusion.13
  2.8 1.9 %collective-permute-start.4 = (f32[288,512]{1,0:T(8,128)S(1)}, f32[288,512]{1,0:T(8,128)S(1)}, u32[]{:S(2)}, u32[]{:S(2)}) collective-permute-start(f32[288,512]{1,0:T(8,128)S(1)} %fusion.13), channel_id=1, source_target_pairs={{0,1},{1,0},{2,3},{3,2},{4,5},{5,4},{6,7},{7,6},{8,9},{9,8},{10,11... | collective-permute-start | bytes 1769480 | tf_op jit(solution)/shard_map/ppermute | solution.py:30
  4.7 0.5 fusion.12
  5.2 1.5 %collective-permute-done.4 = f32[288,512]{1,0:T(8,128)S(1)} collective-permute-done((f32[288,512]{1,0:T(8,128)S(1)}, f32[288,512]{1,0:T(8,128)S(1)}, u32[]{:S(2)}, u32[]{:S(2)}) %collective-permute-start.4) | collective-permute-done | bytes 589856 | tf_op jit(solution)/shard_map/ppermute | solution.py:30
  6.7 0.1 add.71
  6.8 14.6 %all_to_all.25 = f32[4,72,512]{2,1,0:T(8,128)S(1)} all-to-all(f32[4,72,512]{2,1,0:T(8,128)S(1)} %bitcast.43), channel_id=1, replica_groups=mesh['y'=4,'zh'=8,'zl'=2,'x'=4,'core'=2] {'x'}, dimensions={0} | all-to-all | bytes 1179648 | tf_op jit(solution)/shard_map/all_to_all | solution.py:16
  21.4 13.2 %all_gather.3 = bf16[576,512]{1,0:T(8,128)(2,1)S(1)} all-gather(bf16[72,512]{1,0:T(8,128)(2,1)S(1)} %reduce_sum.30), channel_id=1, replica_groups=mesh['y'=4,'zh'=8,'zl'=2,'x'=4,'core'=2] {'x','core'}, dimensions={0}, use_global_device_ids=true | all-gather | bytes 663552 | tf_op jit(solution)/shard_map/all_gather | solution.py:35
  34.6 0.0 copy-done
  34.6 1.4 %convolution_convert_fusion = bf16[512,1408]{1,0:T(8,128)(2,1)S(1)} fusion(bf16[576,512]{1,0:T(8,128)(2,1)S(1)} %all_gather.3, bf16[576,1408]{1,0:T(8,128)(2,1)S(1)} %copy-done), kind=kOutput, calls=%fused_computation | convolution fusion | flops 831193088 | bytes 3653632 | tf_op jit(solution)/shard_map/dot_general | solution.py:58
  36.0 0.1 copy.14
  36.2 26.3 %all_to_all.26 = bf16[8,64,1408]{2,1,0:T(8,128)(2,1)} all-to-all(bf16[8,64,1408]{2,1,0:T(8,128)(2,1)S(1)} %bitcast.42), channel_id=1, replica_groups=mesh['y'=4,'zh'=8,'zl'=2,'x'=4,'core'=2] {'y','zl'}, dimensions={0} | all-to-all | bytes 2883584 | tf_op jit(solution)/shard_map/all_to_all | solution.py:16
  62.4 0.0 copy-start.2
  62.4 0.0 copy-start.3
  62.4 2.3 %reduce_sum.31 = bf16[64,1408]{1,0:T(8,128)(2,1)} reduce(bf16[8,64,1408]{2,1,0:T(8,128)(2,1)} %all_to_all.26, bf16[]{:T(256)} %constant.99.clone.1), dimensions={0}, to_apply=%region_1.2 | reduce | flops 630784 | bytes 1622018 | tf_op jit(solution)/shard_map/reduce_sum | solution.py:20
  64.7 13.8 %all-to-all-start.2 = ((bf16[8,8,1408]{2,1,0:T(8,128)(2,1)}), bf16[8,8,1408]{2,1,0:T(8,128)(2,1)S(1)}, u32[]{:S(2)}, u32[]{:S(2)}) async-start(bf16[8,8,1408]{2,1,0:T(8,128)(2,1)} %bitcast.15), calls=%async_computation.2 | async-start | bytes 360448 | tf_op jit(solution)/shard_map/all_to_all | solution.py:16
  78.6 1.9 %collective-permute-start = (bf16[256,512]{1,0:T(8,128)(2,1)S(1)}, bf16[256,512]{1,0:T(8,128)(2,1)}, u32[]{:S(2)}, u32[]{:S(2)}) collective-permute-start(bf16[256,512]{1,0:T(8,128)(2,1)S(1)} %constant_dynamic-slice_fusion.2), channel_id=1, source_target_pairs={{0,1},{1,0},{2,3},{3,2},{4,5},{5,4},{6,7},{7,6},{8,9},{9,8},{10,11... | collective-permute-start | bytes 786440 | tf_op jit(solution)/shard_map/ppermute | solution.py:43
  80.5 13.4 %all-to-all-done.2 = bf16[8,8,1408]{2,1,0:T(8,128)(2,1)S(1)} async-done(((bf16[8,8,1408]{2,1,0:T(8,128)(2,1)}), bf16[8,8,1408]{2,1,0:T(8,128)(2,1)S(1)}, u32[]{:S(2)}, u32[]{:S(2)}) %all-to-all-start.2) | async-done | bytes 180256 | tf_op jit(solution)/shard_map/all_to_all | solution.py:16
  94.0 0.0 copy-done.2
  94.0 0.0 copy-done.3
  94.0 0.7 divide_convert_fusion
  94.7 0.1 reshape.51
  94.8 0.7 broadcast_in_dim.8
  95.5 5.8 %all-to-all-start.3 = ((bf16[64,8,176]{2,1,0:T(8,128)(2,1)}), bf16[64,8,176]{2,1,0:T(8,128)(2,1)S(1)}, u32[]{:S(2)}, u32[]{:S(2)}) async-start(bf16[64,8,176]{2,1,0:T(8,128)(2,1)} %bitcast.18), calls=%async_computation.3 | async-start | bytes 524288 | tf_op jit(solution)/shard_map/all_to_all | solution.py:16
  101.4 0.0 collective-permute-done
  101.4 0.1 broadcast_select_fusion
  101.5 3.1 %collective-permute-start.3 = (bf16[256,512]{1,0:T(8,128)(2,1)S(1)}, bf16[256,512]{1,0:T(8,128)(2,1)S(1)}, u32[]{:S(2)}, u32[]{:S(2)}) collective-permute-start(bf16[256,512]{1,0:T(8,128)(2,1)S(1)} %broadcast_select_fusion), channel_id=1, source_target_pairs={{0,6},{2,0},{4,2},{6,4},{1,7},{3,1},{5,3},{7,5},{8,14},{10,8},{12,... | collective-permute-start | bytes 786440 | tf_op jit(solution)/shard_map/ppermute | solution.py:48
  104.5 2.8 %collective-permute-start.2 = (bf16[256,512]{1,0:T(8,128)(2,1)S(1)}, bf16[256,512]{1,0:T(8,128)(2,1)S(1)}, u32[]{:S(2)}, u32[]{:S(2)}) collective-permute-start(bf16[256,512]{1,0:T(8,128)(2,1)S(1)} %broadcast_select_fusion), channel_id=1, source_target_pairs={{0,4},{2,6},{4,0},{6,2},{1,5},{3,7},{5,1},{7,3},{8,12},{10,14},{12... | collective-permute-start | bytes 786440 | tf_op jit(solution)/shard_map/ppermute | solution.py:48
  107.3 2.8 %collective-permute-start.1 = (bf16[256,512]{1,0:T(8,128)(2,1)S(1)}, bf16[256,512]{1,0:T(8,128)(2,1)S(1)}, u32[]{:S(2)}, u32[]{:S(2)}) collective-permute-start(bf16[256,512]{1,0:T(8,128)(2,1)S(1)} %broadcast_select_fusion), channel_id=1, source_target_pairs={{0,2},{2,4},{4,6},{6,0},{1,3},{3,5},{5,7},{7,1},{8,10},{10,12},{12... | collective-permute-start | bytes 786440 | tf_op jit(solution)/shard_map/ppermute | solution.py:48
  110.2 2.4 %collective-permute-done.3 = bf16[256,512]{1,0:T(8,128)(2,1)S(1)} collective-permute-done((bf16[256,512]{1,0:T(8,128)(2,1)S(1)}, bf16[256,512]{1,0:T(8,128)(2,1)S(1)}, u32[]{:S(2)}, u32[]{:S(2)}) %collective-permute-start.3) | collective-permute-done | bytes 262176 | tf_op jit(solution)/shard_map/ppermute | solution.py:48
  112.6 4.6 %collective-permute-done.2 = bf16[256,512]{1,0:T(8,128)(2,1)S(1)} collective-permute-done((bf16[256,512]{1,0:T(8,128)(2,1)S(1)}, bf16[256,512]{1,0:T(8,128)(2,1)S(1)}, u32[]{:S(2)}, u32[]{:S(2)}) %collective-permute-start.2) | collective-permute-done | bytes 262176 | tf_op jit(solution)/shard_map/ppermute | solution.py:48
  117.2 3.3 %collective-permute-done.1 = bf16[256,512]{1,0:T(8,128)(2,1)S(1)} collective-permute-done((bf16[256,512]{1,0:T(8,128)(2,1)S(1)}, bf16[256,512]{1,0:T(8,128)(2,1)S(1)}, u32[]{:S(2)}, u32[]{:S(2)}) %collective-permute-start.1) | collective-permute-done | bytes 262176 | tf_op jit(solution)/shard_map/ppermute | solution.py:48
  120.5 0.1 pad_maximum_fusion
  120.6 0.1 dynamic-slice_bitcast_fusion.3
  120.7 0.0 all-to-all-done.3
  120.7 0.5 fusion
  121.2 0.1 copy.20
  121.3 13.0 %all_to_all.27 = bf16[8,128,176]{1,2,0:T(8,128)(2,1)S(1)} all-to-all(bf16[8,128,176]{1,2,0:T(8,128)(2,1)S(1)} %bitcast.47), channel_id=1, replica_groups=mesh['y'=4,'zh'=8,'zl'=2,'x'=4,'core'=2] {'y','zl'}, dimensions={0} | all-to-all | bytes 720896 | tf_op jit(solution)/shard_map/all_to_all | solution.py:16
  134.3 0.9 copy.17
  (4 shorter events, 0.1 us)
Async XLA Ops:
  0.6 34.0 %copy-start = (bf16[576,1408]{1,0:T(8,128)(2,1)S(1)}, bf16[576,1408]{1,0:T(8,128)(2,1)}, u32[]{:S(2)}) copy-start(bf16[576,1408]{1,0:T(8,128)(2,1)} %param.6) | copy-start | bytes 4866052
  0.6 1.7 %copy-start.1 = (bf16[1024,512]{1,0:T(8,128)(2,1)S(1)}, bf16[1024,512]{1,0:T(8,128)(2,1)}, u32[]{:S(2)}) copy-start(bf16[1024,512]{1,0:T(8,128)(2,1)} %param.7) | copy-start | bytes 3145732
  2.8 3.9 %collective-permute-start.4 = (f32[288,512]{1,0:T(8,128)S(1)}, f32[288,512]{1,0:T(8,128)S(1)}, u32[]{:S(2)}, u32[]{:S(2)}) collective-permute-start(f32[288,512]{1,0:T(8,128)S(1)} %fusion.13), channel_id=1, source_target_pairs={{0,1},{1,0},{2,3},{3,2},{4,5},{5,4},{6,7},{7,6},{8,9},{9,8},{10,11... | collective-permute-start | bytes 1769480 | tf_op jit(solution)/shard_map/ppermute | solution.py:30
  62.4 31.6 %copy-start.2 = (f32[8,1408]{1,0:T(8,128)S(1)}, f32[8,1408]{1,0:T(8,128)}, u32[]{:S(2)}) copy-start(f32[8,1408]{1,0:T(8,128)} %param.8) | copy-start | bytes 135172
  62.4 31.6 %copy-start.3 = (f32[8,1408]{1,0:T(8,128)S(1)}, f32[8,1408]{1,0:T(8,128)}, u32[]{:S(2)}) copy-start(f32[8,1408]{1,0:T(8,128)} %param.9) | copy-start | bytes 135172
  64.7 29.2 %all-to-all-start.2 = ((bf16[8,8,1408]{2,1,0:T(8,128)(2,1)}), bf16[8,8,1408]{2,1,0:T(8,128)(2,1)S(1)}, u32[]{:S(2)}, u32[]{:S(2)}) async-start(bf16[8,8,1408]{2,1,0:T(8,128)(2,1)} %bitcast.15), calls=%async_computation.2 | async-start | bytes 360448 | tf_op jit(solution)/shard_map/all_to_all | solution.py:16
  78.6 22.8 %collective-permute-start = (bf16[256,512]{1,0:T(8,128)(2,1)S(1)}, bf16[256,512]{1,0:T(8,128)(2,1)}, u32[]{:S(2)}, u32[]{:S(2)}) collective-permute-start(bf16[256,512]{1,0:T(8,128)(2,1)S(1)} %constant_dynamic-slice_fusion.2), channel_id=1, source_target_pairs={{0,1},{1,0},{2,3},{3,2},{4,5},{5,4},{6,7},{7,6},{8,9},{9,8},{10,11... | collective-permute-start | bytes 786440 | tf_op jit(solution)/shard_map/ppermute | solution.py:43
  95.5 25.2 %all-to-all-start.3 = ((bf16[64,8,176]{2,1,0:T(8,128)(2,1)}), bf16[64,8,176]{2,1,0:T(8,128)(2,1)S(1)}, u32[]{:S(2)}, u32[]{:S(2)}) async-start(bf16[64,8,176]{2,1,0:T(8,128)(2,1)} %bitcast.18), calls=%async_computation.3 | async-start | bytes 524288 | tf_op jit(solution)/shard_map/all_to_all | solution.py:16
  101.5 11.1 %collective-permute-start.3 = (bf16[256,512]{1,0:T(8,128)(2,1)S(1)}, bf16[256,512]{1,0:T(8,128)(2,1)S(1)}, u32[]{:S(2)}, u32[]{:S(2)}) collective-permute-start(bf16[256,512]{1,0:T(8,128)(2,1)S(1)} %broadcast_select_fusion), channel_id=1, source_target_pairs={{0,6},{2,0},{4,2},{6,4},{1,7},{3,1},{5,3},{7,5},{8,14},{10,8},{12,... | collective-permute-start | bytes 786440 | tf_op jit(solution)/shard_map/ppermute | solution.py:48
  104.5 12.6 %collective-permute-start.2 = (bf16[256,512]{1,0:T(8,128)(2,1)S(1)}, bf16[256,512]{1,0:T(8,128)(2,1)S(1)}, u32[]{:S(2)}, u32[]{:S(2)}) collective-permute-start(bf16[256,512]{1,0:T(8,128)(2,1)S(1)} %broadcast_select_fusion), channel_id=1, source_target_pairs={{0,4},{2,6},{4,0},{6,2},{1,5},{3,7},{5,1},{7,3},{8,12},{10,14},{12... | collective-permute-start | bytes 786440 | tf_op jit(solution)/shard_map/ppermute | solution.py:48
  107.3 13.2 %collective-permute-start.1 = (bf16[256,512]{1,0:T(8,128)(2,1)S(1)}, bf16[256,512]{1,0:T(8,128)(2,1)S(1)}, u32[]{:S(2)}, u32[]{:S(2)}) collective-permute-start(bf16[256,512]{1,0:T(8,128)(2,1)S(1)} %broadcast_select_fusion), channel_id=1, source_target_pairs={{0,2},{2,4},{4,6},{6,0},{1,3},{3,5},{5,7},{7,1},{8,10},{10,12},{12... | collective-permute-start | bytes 786440 | tf_op jit(solution)/shard_map/ppermute | solution.py:48

commit v3 on v2

v3 whole, which is shorter than its diff:
```python
import jax
import jax.numpy as jnp
from jax import lax
from jax.experimental import pallas as pl
from jax.experimental.pallas import tpu as pltpu
from jax.sharding import Mesh, PartitionSpec as P

STEP = 100
Y, ZH, ZL, X, C = 4, 8, 2, 4, 2
BF16 = jnp.bfloat16
F32 = jnp.float32
AXES = ("y", "zh", "zl", "x", "core")
DP = ("y", "zh", "zl")
TENSOR = ("x", "core")


def exchange(blocks, axes):
    return lax.all_to_all(blocks, axes, 0, 0)


def sum_blocks(blocks):
    return jnp.sum(blocks.astype(F32), axis=0)


def project(features, bases):
    half = features.shape[0] // C
    first, own_core = pair_place(bases)
    features, first, own_core = lax.optimization_barrier((features, first, own_core))
    core = lax.axis_index("core")
    halves = features.reshape(X, C, half // X, -1)
    theirs = lax.dynamic_index_in_dim(halves, 1 - core, 1, False).reshape(half, -1)
    ours = lax.dynamic_index_in_dim(halves, core, 1, False).reshape(half, -1)
    away = jnp.dot(theirs, bases, preferred_element_type=F32)
    arrived = lax.ppermute(away, "core", [(0, 1), (1, 0)])
    kept = jnp.dot(ours, bases, preferred_element_type=F32)
    kept = lax.optimization_barrier(kept)
    blocks = (kept + arrived).reshape(X, half // X, -1)
    my_tokens = sum_blocks(exchange(blocks, "x")).astype(BF16)
    my_tokens, bases = lax.optimization_barrier((my_tokens, bases))
    block = basis_block_of_pair(bases, first, own_core)
    return lax.all_gather(my_tokens, TENSOR, axis=0, tiled=True), block


def pair_place(bases):
    zh = lax.axis_index("zh")
    return (zh % 4) * (bases.shape[0] // 8 * ZL), lax.axis_index("core") == zh // 4


def basis_block_of_pair(bases, first, own_core):
    rows = bases.shape[0] // 8 * ZL
    piece = lax.dynamic_slice_in_dim(
        bases, first, rows, 0, allow_negative_indices=False
    )
    other = lax.ppermute(piece, "core", [(0, 1), (1, 0)])
    return jnp.where(own_core, piece, other)


def from_all_x(block):
    x = lax.axis_index("x")
    blocks = [block]
    for step in range(1, X):
        pairs = [(i, (i + step) % X) for i in range(X)]
        blocks.append(lax.ppermute(block, "x", pairs))
    stacked = jnp.stack(blocks)
    return jnp.concatenate(
        [lax.dynamic_index_in_dim(stacked, (x - i) % X, 0, False) for i in range(X)]
    )


def adam_kernel(parts_ref, one_ref, two_ref, new_one_ref, new_two_ref, copies_ref):
    reduced = parts_ref[0].astype(F32)
    for place in range(1, ZH):
        reduced += parts_ref[place].astype(F32)
    new_one = 0.9 * one_ref[...] + 0.1 * reduced
    new_two = 0.999 * two_ref[...] + 0.001 * reduced * reduced
    new_one_ref[...] = new_one
    new_two_ref[...] = new_two
    first_fix = 1.0 - 0.9**STEP
    second_fix = 1.0 - 0.999**STEP
    direction = new_one / first_fix / (jnp.sqrt(new_two / second_fix) + 1e-08)
    width = copies_ref.shape[2]
    for part in range(Y * ZL):
        piece = direction[:, part * width : (part + 1) * width].astype(BF16)
        y, zl = part // ZL, part % ZL
        for zh in range(ZH):
            copies_ref[(y * ZH + zh) * ZL + zl] = piece


def per_device(features, out_grads, bases, moment_one, moment_two):
    projected_low, block = project(features, bases)
    partial_sum = lax.dot_general(
        projected_low, out_grads, (((0,), (0,)), ((), ())), preferred_element_type=F32
    ).astype(BF16)
    partial_sum, block = lax.optimization_barrier((partial_sum, block))
    basis_rows = from_all_x(block)
    rank, columns = partial_sum.shape
    own = rank // (Y * ZH * ZL)
    blocks = partial_sum.reshape(Y, ZH, ZL, own, columns).transpose(0, 2, 1, 3, 4)
    blocks = blocks.reshape(Y * ZL, ZH * own, columns)
    near = sum_blocks(exchange(blocks, ("y", "zl"))).astype(BF16)
    arrived = exchange(near.reshape(ZH, own, columns), "zh")
    parts = Y * ZL
    width = columns // parts
    vmem = pl.BlockSpec(memory_space=pltpu.VMEM)
    new_moment_one, new_moment_two, copies = pl.pallas_call(
        adam_kernel,
        in_specs=[vmem] * 3,
        out_specs=[vmem] * 3,
        out_shape=[
            jax.ShapeDtypeStruct((own, columns), F32),
            jax.ShapeDtypeStruct((own, columns), F32),
            jax.ShapeDtypeStruct((parts * ZH, own, width), BF16),
        ],
    )(arrived, moment_one, moment_two)
    my_columns = exchange(copies, DP).reshape(rank, width)
    tile = jnp.dot(basis_rows, my_columns, preferred_element_type=F32).astype(BF16)
    tiles = exchange(tile.reshape(parts, -1, width), ("y", "zl"))
    update = tiles.transpose(1, 0, 2).reshape(-1, columns)
    return (update, new_moment_one, new_moment_two)


def solution(mesh):
    split = Mesh(mesh.devices.reshape(Y, ZH, ZL, X, C), AXES)
    cut = P(DP, TENSOR)
    return jax.shard_map(
        per_device,
        mesh=split,
        in_specs=(cut, cut, P(TENSOR, None), cut, cut),
        out_specs=(cut, cut, cut),
        check_vma=False,
    )
```

time: 136 us -> 135 us (level)
  the two profiles are of different devices: /device:TPU:64 before, /device:TPU:8 now
where the time goes in v3:
time: 135 us
  blocking collectives  95.9 us (71%)
  starting transfers between devices  17.9 us (13%)
  waiting for transfers between devices  12 us (9%)
  local copies, waits for them, and re-layouts  2.93 us (2%)
  matrix products  2.84 us (2%)
  Pallas kernels  1.79 us (1%)
    all_to_all x4, blocking collectives, exchange(): return lax.all_to_all(blocks, axes, 0, 0)  82.7 us
    all_gather x1, blocking collectives, project(): return (lax.all_gather(my_tokens, TENSOR, axis=0, tiled=True), block)  13.2 us
    ppermute x3, waiting for transfers between devices, from_all_x(): blocks.append(lax.ppermute(block, 'x', pairs))  9.26 us
    ppermute x3, starting transfers between devices, from_all_x(): blocks.append(lax.ppermute(block, 'x', pairs))  8.61 us
    all_to_all x1, starting transfers between devices, exchange(): return lax.all_to_all(blocks, axes, 0, 0)  5.44 us
  transfers between devices with their start and end apart: 6, of which 5 were waited for; matrix products, arithmetic and copies ran while one was open for 2% of the time, Pallas kernels for 0%

profile of v3, /device:TPU:8, one launch (start us, length us, event | category | flops | bytes accessed | tf_op | source)
XLA Modules:
  0.0 134.8 jit_solution(2259248458969995867)
XLA Ops:
  0.6 0.0 copy-start
  0.6 0.0 copy-start.1
  0.7 1.5 %constant_dynamic-slice_fusion.1 = (bf16[4,1,72,1024]{3,2,1,0:T(8,128)(2,1)S(1)}, bf16[4,1,72,1024]{3,2,1,0:T(8,128)(2,1)S(1)}) fusion(bf16[4,2,72,1024]{3,2,1,0:T(8,128)(2,1)} %bitcast.45, s32[]{:T(128)S(6)} %select_n.58, s32[]{:T(128)S(6)} %select_n.57), kind=kLoop, calls=%fused_computation.19 | loop fusion | bytes 2359304 | tf_op jit(solution)/shard_map/jit(dynamic_index_in_dim)/dynamic_slice | solution.py:31
  2.2 0.2 copy-done.1
  2.3 0.5 fusion.11
  2.8 1.9 %collective-permute-start = (f32[288,512]{1,0:T(8,128)S(1)}, f32[288,512]{1,0:T(8,128)S(1)}, u32[]{:S(2)}, u32[]{:S(2)}) collective-permute-start(f32[288,512]{1,0:T(8,128)S(1)} %fusion.11), channel_id=1, source_target_pairs={{0,1},{1,0},{2,3},{3,2},{4,5},{5,4},{6,7},{7,6},{8,9},{9,8},{10,11... | collective-permute-start | bytes 1769480 | tf_op jit(solution)/shard_map/ppermute | solution.py:34
  4.7 0.5 fusion.10
  5.2 1.5 %collective-permute-done = f32[288,512]{1,0:T(8,128)S(1)} collective-permute-done((f32[288,512]{1,0:T(8,128)S(1)}, f32[288,512]{1,0:T(8,128)S(1)}, u32[]{:S(2)}, u32[]{:S(2)}) %collective-permute-start) | collective-permute-done | bytes 589856 | tf_op jit(solution)/shard_map/ppermute | solution.py:34
  6.7 0.1 add.47
  6.8 14.6 %all_to_all.25 = f32[4,72,512]{2,1,0:T(8,128)S(1)} all-to-all(f32[4,72,512]{2,1,0:T(8,128)S(1)} %bitcast.39), channel_id=1, replica_groups=mesh['y'=4,'zh'=8,'zl'=2,'x'=4,'core'=2] {'x'}, dimensions={0} | all-to-all | bytes 1179648 | tf_op jit(solution)/shard_map/all_to_all | solution.py:18
  21.4 0.1 constant_dynamic-slice_fusion
  21.5 1.9 %collective-permute-start.1 = (bf16[256,512]{1,0:T(8,128)(2,1)S(1)}, bf16[256,512]{1,0:T(8,128)(2,1)S(1)}, u32[]{:S(2)}, u32[]{:S(2)}) collective-permute-start(bf16[256,512]{1,0:T(8,128)(2,1)S(1)} %constant_dynamic-slice_fusion), channel_id=1, source_target_pairs={{0,1},{1,0},{2,3},{3,2},{4,5},{5,4},{6,7},{7,6},{8,9},{9,8},{10,11... | collective-permute-start | bytes 786440 | tf_op jit(solution)/shard_map/ppermute | solution.py:54
  23.4 13.2 %all_gather.3 = bf16[576,512]{1,0:T(8,128)(2,1)S(1)} all-gather(bf16[72,512]{1,0:T(8,128)(2,1)S(1)} %reduce_sum.21), channel_id=1, replica_groups=mesh['y'=4,'zh'=8,'zl'=2,'x'=4,'core'=2] {'x','core'}, dimensions={0}, use_global_device_ids=true | all-gather | bytes 663552 | tf_op jit(solution)/shard_map/all_gather | solution.py:41
  36.6 0.0 copy-done
  36.6 1.4 %convolution_convert_fusion = bf16[512,1408]{1,0:T(8,128)(2,1)S(1)} fusion(bf16[576,512]{1,0:T(8,128)(2,1)S(1)} %all_gather.3, bf16[576,1408]{1,0:T(8,128)(2,1)S(1)} %copy-done), kind=kOutput, calls=%fused_computation | convolution fusion | flops 831193088 | bytes 3653632 | tf_op jit(solution)/shard_map/dot_general | solution.py:91
  38.0 0.0 collective-permute-done.1
  38.1 0.1 broadcast_select_fusion
  38.2 0.1 copy.9
  38.3 26.0 %all_to_all.26 = bf16[8,64,1408]{2,1,0:T(8,128)(2,1)S(1)} all-to-all(bf16[8,64,1408]{2,1,0:T(8,128)(2,1)S(1)} %bitcast.38), channel_id=1, replica_groups=mesh['y'=4,'zh'=8,'zl'=2,'x'=4,'core'=2] {'y','zl'}, dimensions={0} | all-to-all | bytes 2883584 | tf_op jit(solution)/shard_map/all_to_all | solution.py:18
  64.3 0.2 reduce_sum.22
  64.5 30.6 %all_to_all.27.parts_ref = bf16[8,8,1408]{2,1,0:T(8,128)(2,1)} all-to-all(bf16[8,8,1408]{2,1,0:T(8,128)(2,1)S(1)} %bitcast.47), channel_id=1, replica_groups=mesh['y'=4,'zh'=8,'zl'=2,'x'=4,'core'=2] {'zh'}, dimensions={0} | all-to-all | bytes 360448 | tf_op jit(solution)/shard_map/all_to_all | solution.py:18
  95.1 1.8 %shard_map.76 = (f32[8,1408]{1,0:T(8,128)}, f32[8,1408]{1,0:T(8,128)}, bf16[64,8,176]{2,1,0:T(8,128)(2,1)}) custom-call(bf16[8,8,1408]{2,1,0:T(8,128)(2,1)} %all_to_all.27.parts_ref, f32[8,1408]{1,0:T(8,128)} %one_ref.1, f32[8,1408]{1,0:T(8,128)} %two_ref.1), custom_call_target="tpu_custom_call" | custom-call | tf_op jit(solution)/shard_map/pallas_call | solution.py:105
  96.9 5.4 %all-to-all-start.3 = ((bf16[64,8,176]{2,1,0:T(8,128)(2,1)}), bf16[64,8,176]{2,1,0:T(8,128)(2,1)S(1)}, u32[]{:S(2)}, u32[]{:S(2)}) async-start(bf16[64,8,176]{2,1,0:T(8,128)(2,1)} %get-tuple-element.20), calls=%async_computation.3 | async-start | bytes 524288 | tf_op jit(solution)/shard_map/all_to_all | solution.py:18
  102.3 3.1 %collective-permute-start.4 = (bf16[256,512]{1,0:T(8,128)(2,1)S(1)}, bf16[256,512]{1,0:T(8,128)(2,1)S(1)}, u32[]{:S(2)}, u32[]{:S(2)}) collective-permute-start(bf16[256,512]{1,0:T(8,128)(2,1)S(1)} %broadcast_select_fusion), channel_id=1, source_target_pairs={{0,6},{2,0},{4,2},{6,4},{1,7},{3,1},{5,3},{7,5},{8,14},{10,8},{12,... | collective-permute-start | bytes 786440 | tf_op jit(solution)/shard_map/ppermute | solution.py:63
  105.4 2.8 %collective-permute-start.3 = (bf16[256,512]{1,0:T(8,128)(2,1)S(1)}, bf16[256,512]{1,0:T(8,128)(2,1)S(1)}, u32[]{:S(2)}, u32[]{:S(2)}) collective-permute-start(bf16[256,512]{1,0:T(8,128)(2,1)S(1)} %broadcast_select_fusion), channel_id=1, source_target_pairs={{0,4},{2,6},{4,0},{6,2},{1,5},{3,7},{5,1},{7,3},{8,12},{10,14},{12... | collective-permute-start | bytes 786440 | tf_op jit(solution)/shard_map/ppermute | solution.py:63
  108.2 2.8 %collective-permute-start.2 = (bf16[256,512]{1,0:T(8,128)(2,1)S(1)}, bf16[256,512]{1,0:T(8,128)(2,1)S(1)}, u32[]{:S(2)}, u32[]{:S(2)}) collective-permute-start(bf16[256,512]{1,0:T(8,128)(2,1)S(1)} %broadcast_select_fusion), channel_id=1, source_target_pairs={{0,2},{2,4},{4,6},{6,0},{1,3},{3,5},{5,7},{7,1},{8,10},{10,12},{12... | collective-permute-start | bytes 786440 | tf_op jit(solution)/shard_map/ppermute | solution.py:63
  111.0 2.1 %collective-permute-done.4 = bf16[256,512]{1,0:T(8,128)(2,1)S(1)} collective-permute-done((bf16[256,512]{1,0:T(8,128)(2,1)S(1)}, bf16[256,512]{1,0:T(8,128)(2,1)S(1)}, u32[]{:S(2)}, u32[]{:S(2)}) %collective-permute-start.4) | collective-permute-done | bytes 262176 | tf_op jit(solution)/shard_map/ppermute | solution.py:63
  113.2 4.6 %collective-permute-done.3 = bf16[256,512]{1,0:T(8,128)(2,1)S(1)} collective-permute-done((bf16[256,512]{1,0:T(8,128)(2,1)S(1)}, bf16[256,512]{1,0:T(8,128)(2,1)S(1)}, u32[]{:S(2)}, u32[]{:S(2)}) %collective-permute-start.3) | collective-permute-done | bytes 262176 | tf_op jit(solution)/shard_map/ppermute | solution.py:63
  117.8 2.5 %collective-permute-done.2 = bf16[256,512]{1,0:T(8,128)(2,1)S(1)} collective-permute-done((bf16[256,512]{1,0:T(8,128)(2,1)S(1)}, bf16[256,512]{1,0:T(8,128)(2,1)S(1)}, u32[]{:S(2)}, u32[]{:S(2)}) %collective-permute-start.2) | collective-permute-done | bytes 262176 | tf_op jit(solution)/shard_map/ppermute | solution.py:63
  120.3 0.1 pad_maximum_fusion
  120.4 0.1 dynamic-slice_bitcast_fusion.3
  120.5 1.3 all-to-all-done.3
  121.8 0.5 fusion
  122.3 0.1 copy.14
  122.4 11.5 %all_to_all.28 = bf16[8,128,176]{1,2,0:T(8,128)(2,1)S(1)} all-to-all(bf16[8,128,176]{1,2,0:T(8,128)(2,1)S(1)} %bitcast.43), channel_id=1, replica_groups=mesh['y'=4,'zh'=8,'zl'=2,'x'=4,'core'=2] {'y','zl'}, dimensions={0} | all-to-all | bytes 720896 | tf_op jit(solution)/shard_map/all_to_all | solution.py:18
  133.9 0.9 copy.11
  (1 shorter events, 0.0 us)
Async XLA Ops:
  0.6 36.0 %copy-start = (bf16[576,1408]{1,0:T(8,128)(2,1)S(1)}, bf16[576,1408]{1,0:T(8,128)(2,1)}, u32[]{:S(2)}) copy-start(bf16[576,1408]{1,0:T(8,128)(2,1)} %param.6) | copy-start | bytes 4866052
  0.6 1.7 %copy-start.1 = (bf16[1024,512]{1,0:T(8,128)(2,1)S(1)}, bf16[1024,512]{1,0:T(8,128)(2,1)}, u32[]{:S(2)}) copy-start(bf16[1024,512]{1,0:T(8,128)(2,1)} %param.7) | copy-start | bytes 3145732
  2.8 3.9 %collective-permute-start = (f32[288,512]{1,0:T(8,128)S(1)}, f32[288,512]{1,0:T(8,128)S(1)}, u32[]{:S(2)}, u32[]{:S(2)}) collective-permute-start(f32[288,512]{1,0:T(8,128)S(1)} %fusion.11), channel_id=1, source_target_pairs={{0,1},{1,0},{2,3},{3,2},{4,5},{5,4},{6,7},{7,6},{8,9},{9,8},{10,11... | collective-permute-start | bytes 1769480 | tf_op jit(solution)/shard_map/ppermute | solution.py:34
  21.5 16.5 %collective-permute-start.1 = (bf16[256,512]{1,0:T(8,128)(2,1)S(1)}, bf16[256,512]{1,0:T(8,128)(2,1)S(1)}, u32[]{:S(2)}, u32[]{:S(2)}) collective-permute-start(bf16[256,512]{1,0:T(8,128)(2,1)S(1)} %constant_dynamic-slice_fusion), channel_id=1, source_target_pairs={{0,1},{1,0},{2,3},{3,2},{4,5},{5,4},{6,7},{7,6},{8,9},{9,8},{10,11... | collective-permute-start | bytes 786440 | tf_op jit(solution)/shard_map/ppermute | solution.py:54
  96.9 24.9 %all-to-all-start.3 = ((bf16[64,8,176]{2,1,0:T(8,128)(2,1)}), bf16[64,8,176]{2,1,0:T(8,128)(2,1)S(1)}, u32[]{:S(2)}, u32[]{:S(2)}) async-start(bf16[64,8,176]{2,1,0:T(8,128)(2,1)} %get-tuple-element.20), calls=%async_computation.3 | async-start | bytes 524288 | tf_op jit(solution)/shard_map/all_to_all | solution.py:18
  102.3 10.9 %collective-permute-start.4 = (bf16[256,512]{1,0:T(8,128)(2,1)S(1)}, bf16[256,512]{1,0:T(8,128)(2,1)S(1)}, u32[]{:S(2)}, u32[]{:S(2)}) collective-permute-start(bf16[256,512]{1,0:T(8,128)(2,1)S(1)} %broadcast_select_fusion), channel_id=1, source_target_pairs={{0,6},{2,0},{4,2},{6,4},{1,7},{3,1},{5,3},{7,5},{8,14},{10,8},{12,... | collective-permute-start | bytes 786440 | tf_op jit(solution)/shard_map/ppermute | solution.py:63
  105.4 12.4 %collective-permute-start.3 = (bf16[256,512]{1,0:T(8,128)(2,1)S(1)}, bf16[256,512]{1,0:T(8,128)(2,1)S(1)}, u32[]{:S(2)}, u32[]{:S(2)}) collective-permute-start(bf16[256,512]{1,0:T(8,128)(2,1)S(1)} %broadcast_select_fusion), channel_id=1, source_target_pairs={{0,4},{2,6},{4,0},{6,2},{1,5},{3,7},{5,1},{7,3},{8,12},{10,14},{12... | collective-permute-start | bytes 786440 | tf_op jit(solution)/shard_map/ppermute | solution.py:63
  108.2 12.1 %collective-permute-start.2 = (bf16[256,512]{1,0:T(8,128)(2,1)S(1)}, bf16[256,512]{1,0:T(8,128)(2,1)S(1)}, u32[]{:S(2)}, u32[]{:S(2)}) collective-permute-start(bf16[256,512]{1,0:T(8,128)(2,1)S(1)} %broadcast_select_fusion), channel_id=1, source_target_pairs={{0,2},{2,4},{4,6},{6,0},{1,3},{3,5},{5,7},{7,1},{8,10},{10,12},{12... | collective-permute-start | bytes 786440 | tf_op jit(solution)/shard_map/ppermute | solution.py:63

commit v4 on v3

--- a/solution.py
+++ b/solution.py
@@ -9,8 +9,8 @@
 Y, ZH, ZL, X, C = 4, 8, 2, 4, 2
 BF16 = jnp.bfloat16
 F32 = jnp.float32
-AXES = ("y", "zh", "zl", "x", "core")
-DP = ("y", "zh", "zl")
+AXES = ("y", "za", "zb", "zl", "x", "core")
+DP = ("y", "za", "zb", "zl")
 TENSOR = ("x", "core")
 
 
@@ -42,7 +42,7 @@
 
 
 def pair_place(bases):
-    zh = lax.axis_index("zh")
+    zh = lax.axis_index(("za", "zb"))
     return (zh % 4) * (bases.shape[0] // 8 * ZL), lax.axis_index("core") == zh // 4
 
 
@@ -95,10 +95,11 @@
     basis_rows = from_all_x(block)
     rank, columns = partial_sum.shape
     own = rank // (Y * ZH * ZL)
-    blocks = partial_sum.reshape(Y, ZH, ZL, own, columns).transpose(0, 2, 1, 3, 4)
+    blocks = partial_sum.reshape(Y, ZH // 2, 2, ZL, own, columns)
+    blocks = blocks.transpose(0, 3, 2, 1, 4, 5)
     blocks = blocks.reshape(Y * ZL, ZH * own, columns)
     near = sum_blocks(exchange(blocks, ("y", "zl"))).astype(BF16)
-    arrived = exchange(near.reshape(ZH, own, columns), "zh")
+    arrived = exchange(near.reshape(ZH, own, columns), ("zb", "za"))
     parts = Y * ZL
     width = columns // parts
     vmem = pl.BlockSpec(memory_space=pltpu.VMEM)
@@ -120,7 +121,7 @@
 
 
 def solution(mesh):
-    split = Mesh(mesh.devices.reshape(Y, ZH, ZL, X, C), AXES)
+    split = Mesh(mesh.devices.reshape(Y, ZH // 2, 2, ZL, X, C), AXES)
     cut = P(DP, TENSOR)
     return jax.shard_map(
         per_device,

time: 135 us -> 136 us (level)
  blocking collectives: 95.9 us -> 93.2 us
  starting transfers between devices: 17.9 us -> 20.1 us
    all_to_all x4, blocking collectives: 82.7 us -> 80 us  [exchange(): return lax.all_to_all(blocks, axes, 0, 0)]
    all_to_all x1, starting transfers between devices: 5.44 us -> 7.69 us  [exchange(): return lax.all_to_all(blocks, axes, 0, 0)]
where the time goes in v4:
time: 136 us; the launch traced here: 135 us
  blocking collectives  93.2 us (69%)
  starting transfers between devices  20.1 us (15%)
  waiting for transfers between devices  12.8 us (9%)
  local copies, waits for them, and re-layouts  2.96 us (2%)
  matrix products  2.84 us (2%)
  Pallas kernels  1.79 us (1%)
    all_to_all x4, blocking collectives, exchange(): return lax.all_to_all(blocks, axes, 0, 0)  80 us
    all_gather x1, blocking collectives, project(): return (lax.all_gather(my_tokens, TENSOR, axis=0, tiled=True), block)  13.2 us
    ppermute x3, waiting for transfers between devices, from_all_x(): blocks.append(lax.ppermute(block, 'x', pairs))  9.9 us
    ppermute x3, starting transfers between devices, from_all_x(): blocks.append(lax.ppermute(block, 'x', pairs))  8.61 us
    all_to_all x1, starting transfers between devices, exchange(): return lax.all_to_all(blocks, axes, 0, 0)  7.69 us
  transfers between devices with their start and end apart: 6, of which 5 were waited for; matrix products, arithmetic and copies ran while one was open for 2% of the time, Pallas kernels for 0%

profile of v4, /device:TPU:8, one launch (start us, length us, event | category | flops | bytes accessed | tf_op | source)
XLA Modules:
  0.0 135.2 jit_solution(7313616248071939483)
XLA Ops:
  0.6 0.0 copy-start
  0.6 0.0 copy-start.1
  0.7 1.5 %constant_dynamic-slice_fusion.1 = (bf16[4,1,72,1024]{3,2,1,0:T(8,128)(2,1)S(1)}, bf16[4,1,72,1024]{3,2,1,0:T(8,128)(2,1)S(1)}) fusion(bf16[4,2,72,1024]{3,2,1,0:T(8,128)(2,1)} %bitcast.45, s32[]{:T(128)S(6)} %select_n.58, s32[]{:T(128)S(6)} %select_n.57), kind=kLoop, calls=%fused_computation.19 | loop fusion | bytes 2359304 | tf_op jit(solution)/shard_map/jit(dynamic_index_in_dim)/dynamic_slice | solution.py:31
  2.2 0.1 copy-done.1
  2.3 0.5 fusion.11
  2.8 1.9 %collective-permute-start = (f32[288,512]{1,0:T(8,128)S(1)}, f32[288,512]{1,0:T(8,128)S(1)}, u32[]{:S(2)}, u32[]{:S(2)}) collective-permute-start(f32[288,512]{1,0:T(8,128)S(1)} %fusion.11), channel_id=1, source_target_pairs={{0,1},{1,0},{2,3},{3,2},{4,5},{5,4},{6,7},{7,6},{8,9},{9,8},{10,11... | collective-permute-start | bytes 1769480 | tf_op jit(solution)/shard_map/ppermute | solution.py:34
  4.7 0.5 fusion.10
  5.2 1.5 %collective-permute-done = f32[288,512]{1,0:T(8,128)S(1)} collective-permute-done((f32[288,512]{1,0:T(8,128)S(1)}, f32[288,512]{1,0:T(8,128)S(1)}, u32[]{:S(2)}, u32[]{:S(2)}) %collective-permute-start) | collective-permute-done | bytes 589856 | tf_op jit(solution)/shard_map/ppermute | solution.py:34
  6.7 0.1 add.51
  6.8 14.6 %all_to_all.25 = f32[4,72,512]{2,1,0:T(8,128)S(1)} all-to-all(f32[4,72,512]{2,1,0:T(8,128)S(1)} %bitcast.39), channel_id=1, replica_groups=mesh['y'=4,'za'=4,'zb'=2,'zl'=2,'x'=4,'core'=2] {'x'}, dimensions={0} | all-to-all | bytes 1179648 | tf_op jit(solution)/shard_map/all_to_all | solution.py:18
  21.4 0.1 constant_dynamic-slice_fusion
  21.5 1.9 %collective-permute-start.1 = (bf16[256,512]{1,0:T(8,128)(2,1)S(1)}, bf16[256,512]{1,0:T(8,128)(2,1)S(1)}, u32[]{:S(2)}, u32[]{:S(2)}) collective-permute-start(bf16[256,512]{1,0:T(8,128)(2,1)S(1)} %constant_dynamic-slice_fusion), channel_id=1, source_target_pairs={{0,1},{1,0},{2,3},{3,2},{4,5},{5,4},{6,7},{7,6},{8,9},{9,8},{10,11... | collective-permute-start | bytes 786440 | tf_op jit(solution)/shard_map/ppermute | solution.py:54
  23.4 13.2 %all_gather.3 = bf16[576,512]{1,0:T(8,128)(2,1)S(1)} all-gather(bf16[72,512]{1,0:T(8,128)(2,1)S(1)} %reduce_sum.21), channel_id=1, replica_groups=mesh['y'=4,'za'=4,'zb'=2,'zl'=2,'x'=4,'core'=2] {'x','core'}, dimensions={0}, use_global_device_ids=true | all-gather | bytes 663552 | tf_op jit(solution)/shard_map/all_gather | solution.py:41
  36.6 0.0 copy-done
  36.6 1.4 %convolution_convert_fusion = bf16[512,1408]{1,0:T(8,128)(2,1)S(1)} fusion(bf16[576,512]{1,0:T(8,128)(2,1)S(1)} %all_gather.3, bf16[576,1408]{1,0:T(8,128)(2,1)S(1)} %copy-done), kind=kOutput, calls=%fused_computation | convolution fusion | flops 831193088 | bytes 3653632 | tf_op jit(solution)/shard_map/dot_general | solution.py:91
  38.0 0.0 collective-permute-done.1
  38.1 0.1 broadcast_select_fusion
  38.2 0.2 copy.9
  38.3 26.0 %all_to_all.26 = bf16[8,64,1408]{2,1,0:T(8,128)(2,1)S(1)} all-to-all(bf16[8,64,1408]{2,1,0:T(8,128)(2,1)S(1)} %bitcast.38), channel_id=1, replica_groups=mesh['y'=4,'za'=4,'zb'=2,'zl'=2,'x'=4,'core'=2] {'y','zl'}, dimensions={0} | all-to-all | bytes 2883584 | tf_op jit(solution)/shard_map/all_to_all | solution.py:18
  64.3 0.2 reduce_sum.22
  64.5 28.0 %all_to_all.27.parts_ref = bf16[8,8,1408]{2,1,0:T(8,128)(2,1)} all-to-all(bf16[8,8,1408]{2,1,0:T(8,128)(2,1)S(1)} %bitcast.47), channel_id=1, replica_groups=mesh['y'=4,'za'=4,'zb'=2,'zl'=2,'x'=4,'core'=2] {'zb','za'}, dimensions={0} | all-to-all | bytes 360448 | tf_op jit(solution)/shard_map/all_to_all | solution.py:18
  92.6 1.8 %shard_map.76 = (f32[8,1408]{1,0:T(8,128)}, f32[8,1408]{1,0:T(8,128)}, bf16[64,8,176]{2,1,0:T(8,128)(2,1)}) custom-call(bf16[8,8,1408]{2,1,0:T(8,128)(2,1)} %all_to_all.27.parts_ref, f32[8,1408]{1,0:T(8,128)} %one_ref.1, f32[8,1408]{1,0:T(8,128)} %two_ref.1), custom_call_target="tpu_custom_call" | custom-call | tf_op jit(solution)/shard_map/pallas_call | solution.py:106
  94.4 7.7 %all-to-all-start.3 = ((bf16[64,8,176]{2,1,0:T(8,128)(2,1)}), bf16[64,8,176]{2,1,0:T(8,128)(2,1)S(1)}, u32[]{:S(2)}, u32[]{:S(2)}) async-start(bf16[64,8,176]{2,1,0:T(8,128)(2,1)} %get-tuple-element.20), calls=%async_computation.3 | async-start | bytes 524288 | tf_op jit(solution)/shard_map/all_to_all | solution.py:18
  102.1 3.1 %collective-permute-start.4 = (bf16[256,512]{1,0:T(8,128)(2,1)S(1)}, bf16[256,512]{1,0:T(8,128)(2,1)S(1)}, u32[]{:S(2)}, u32[]{:S(2)}) collective-permute-start(bf16[256,512]{1,0:T(8,128)(2,1)S(1)} %broadcast_select_fusion), channel_id=1, source_target_pairs={{0,6},{2,0},{4,2},{6,4},{1,7},{3,1},{5,3},{7,5},{8,14},{10,8},{12,... | collective-permute-start | bytes 786440 | tf_op jit(solution)/shard_map/ppermute | solution.py:63
  105.1 2.8 %collective-permute-start.3 = (bf16[256,512]{1,0:T(8,128)(2,1)S(1)}, bf16[256,512]{1,0:T(8,128)(2,1)S(1)}, u32[]{:S(2)}, u32[]{:S(2)}) collective-permute-start(bf16[256,512]{1,0:T(8,128)(2,1)S(1)} %broadcast_select_fusion), channel_id=1, source_target_pairs={{0,4},{2,6},{4,0},{6,2},{1,5},{3,7},{5,1},{7,3},{8,12},{10,14},{12... | collective-permute-start | bytes 786440 | tf_op jit(solution)/shard_map/ppermute | solution.py:63
  107.9 2.8 %collective-permute-start.2 = (bf16[256,512]{1,0:T(8,128)(2,1)S(1)}, bf16[256,512]{1,0:T(8,128)(2,1)S(1)}, u32[]{:S(2)}, u32[]{:S(2)}) collective-permute-start(bf16[256,512]{1,0:T(8,128)(2,1)S(1)} %broadcast_select_fusion), channel_id=1, source_target_pairs={{0,2},{2,4},{4,6},{6,0},{1,3},{3,5},{5,7},{7,1},{8,10},{10,12},{12... | collective-permute-start | bytes 786440 | tf_op jit(solution)/shard_map/ppermute | solution.py:63
  110.8 2.4 %collective-permute-done.4 = bf16[256,512]{1,0:T(8,128)(2,1)S(1)} collective-permute-done((bf16[256,512]{1,0:T(8,128)(2,1)S(1)}, bf16[256,512]{1,0:T(8,128)(2,1)S(1)}, u32[]{:S(2)}, u32[]{:S(2)}) %collective-permute-start.4) | collective-permute-done | bytes 262176 | tf_op jit(solution)/shard_map/ppermute | solution.py:63
  113.2 4.4 %collective-permute-done.3 = bf16[256,512]{1,0:T(8,128)(2,1)S(1)} collective-permute-done((bf16[256,512]{1,0:T(8,128)(2,1)S(1)}, bf16[256,512]{1,0:T(8,128)(2,1)S(1)}, u32[]{:S(2)}, u32[]{:S(2)}) %collective-permute-start.3) | collective-permute-done | bytes 262176 | tf_op jit(solution)/shard_map/ppermute | solution.py:63
  117.6 3.1 %collective-permute-done.2 = bf16[256,512]{1,0:T(8,128)(2,1)S(1)} collective-permute-done((bf16[256,512]{1,0:T(8,128)(2,1)S(1)}, bf16[256,512]{1,0:T(8,128)(2,1)S(1)}, u32[]{:S(2)}, u32[]{:S(2)}) %collective-permute-start.2) | collective-permute-done | bytes 262176 | tf_op jit(solution)/shard_map/ppermute | solution.py:63
  120.7 0.1 pad_maximum_fusion
  120.8 0.1 dynamic-slice_bitcast_fusion.3
  120.9 1.4 %all-to-all-done.3 = bf16[64,8,176]{2,1,0:T(8,128)(2,1)S(1)} async-done(((bf16[64,8,176]{2,1,0:T(8,128)(2,1)}), bf16[64,8,176]{2,1,0:T(8,128)(2,1)S(1)}, u32[]{:S(2)}, u32[]{:S(2)}) %all-to-all-start.3) | async-done | bytes 180256 | tf_op jit(solution)/shard_map/all_to_all | solution.py:18
  122.3 0.5 fusion
  122.8 0.1 copy.14
  122.8 11.4 %all_to_all.28 = bf16[8,128,176]{1,2,0:T(8,128)(2,1)S(1)} all-to-all(bf16[8,128,176]{1,2,0:T(8,128)(2,1)S(1)} %bitcast.43), channel_id=1, replica_groups=mesh['y'=4,'za'=4,'zb'=2,'zl'=2,'x'=4,'core'=2] {'y','zl'}, dimensions={0} | all-to-all | bytes 720896 | tf_op jit(solution)/shard_map/all_to_all | solution.py:18
  134.3 0.9 copy.11
  (1 shorter events, 0.0 us)
Async XLA Ops:
  0.6 36.0 %copy-start = (bf16[576,1408]{1,0:T(8,128)(2,1)S(1)}, bf16[576,1408]{1,0:T(8,128)(2,1)}, u32[]{:S(2)}) copy-start(bf16[576,1408]{1,0:T(8,128)(2,1)} %param.6) | copy-start | bytes 4866052
  0.6 1.7 %copy-start.1 = (bf16[1024,512]{1,0:T(8,128)(2,1)S(1)}, bf16[1024,512]{1,0:T(8,128)(2,1)}, u32[]{:S(2)}) copy-start(bf16[1024,512]{1,0:T(8,128)(2,1)} %param.7) | copy-start | bytes 3145732
  2.8 3.9 %collective-permute-start = (f32[288,512]{1,0:T(8,128)S(1)}, f32[288,512]{1,0:T(8,128)S(1)}, u32[]{:S(2)}, u32[]{:S(2)}) collective-permute-start(f32[288,512]{1,0:T(8,128)S(1)} %fusion.11), channel_id=1, source_target_pairs={{0,1},{1,0},{2,3},{3,2},{4,5},{5,4},{6,7},{7,6},{8,9},{9,8},{10,11... | collective-permute-start | bytes 1769480 | tf_op jit(solution)/shard_map/ppermute | solution.py:34
  21.5 16.5 %collective-permute-start.1 = (bf16[256,512]{1,0:T(8,128)(2,1)S(1)}, bf16[256,512]{1,0:T(8,128)(2,1)S(1)}, u32[]{:S(2)}, u32[]{:S(2)}) collective-permute-start(bf16[256,512]{1,0:T(8,128)(2,1)S(1)} %constant_dynamic-slice_fusion), channel_id=1, source_target_pairs={{0,1},{1,0},{2,3},{3,2},{4,5},{5,4},{6,7},{7,6},{8,9},{9,8},{10,11... | collective-permute-start | bytes 786440 | tf_op jit(solution)/shard_map/ppermute | solution.py:54
  94.4 27.9 %all-to-all-start.3 = ((bf16[64,8,176]{2,1,0:T(8,128)(2,1)}), bf16[64,8,176]{2,1,0:T(8,128)(2,1)S(1)}, u32[]{:S(2)}, u32[]{:S(2)}) async-start(bf16[64,8,176]{2,1,0:T(8,128)(2,1)} %get-tuple-element.20), calls=%async_computation.3 | async-start | bytes 524288 | tf_op jit(solution)/shard_map/all_to_all | solution.py:18
  102.1 11.1 %collective-permute-start.4 = (bf16[256,512]{1,0:T(8,128)(2,1)S(1)}, bf16[256,512]{1,0:T(8,128)(2,1)S(1)}, u32[]{:S(2)}, u32[]{:S(2)}) collective-permute-start(bf16[256,512]{1,0:T(8,128)(2,1)S(1)} %broadcast_select_fusion), channel_id=1, source_target_pairs={{0,6},{2,0},{4,2},{6,4},{1,7},{3,1},{5,3},{7,5},{8,14},{10,8},{12,... | collective-permute-start | bytes 786440 | tf_op jit(solution)/shard_map/ppermute | solution.py:63
  105.1 12.4 %collective-permute-start.3 = (bf16[256,512]{1,0:T(8,128)(2,1)S(1)}, bf16[256,512]{1,0:T(8,128)(2,1)S(1)}, u32[]{:S(2)}, u32[]{:S(2)}) collective-permute-start(bf16[256,512]{1,0:T(8,128)(2,1)S(1)} %broadcast_select_fusion), channel_id=1, source_target_pairs={{0,4},{2,6},{4,0},{6,2},{1,5},{3,7},{5,1},{7,3},{8,12},{10,14},{12... | collective-permute-start | bytes 786440 | tf_op jit(solution)/shard_map/ppermute | solution.py:63
  107.9 12.8 %collective-permute-start.2 = (bf16[256,512]{1,0:T(8,128)(2,1)S(1)}, bf16[256,512]{1,0:T(8,128)(2,1)S(1)}, u32[]{:S(2)}, u32[]{:S(2)}) collective-permute-start(bf16[256,512]{1,0:T(8,128)(2,1)S(1)} %broadcast_select_fusion), channel_id=1, source_target_pairs={{0,2},{2,4},{4,6},{6,0},{1,3},{3,5},{5,7},{7,1},{8,10},{10,12},{12... | collective-permute-start | bytes 786440 | tf_op jit(solution)/shard_map/ppermute | solution.py:63

commit v5 on v3

--- a/solution.py
+++ b/solution.py
@@ -37,8 +37,8 @@
     blocks = (kept + arrived).reshape(X, half // X, -1)
     my_tokens = sum_blocks(exchange(blocks, "x")).astype(BF16)
     my_tokens, bases = lax.optimization_barrier((my_tokens, bases))
-    block = basis_block_of_pair(bases, first, own_core)
-    return lax.all_gather(my_tokens, TENSOR, axis=0, tiled=True), block
+    pieces = basis_pieces_of_pair(bases, first) + (own_core,)
+    return lax.all_gather(my_tokens, TENSOR, axis=0, tiled=True), pieces
 
 
 def pair_place(bases):
@@ -46,13 +46,12 @@
     return (zh % 4) * (bases.shape[0] // 8 * ZL), lax.axis_index("core") == zh // 4
 
 
-def basis_block_of_pair(bases, first, own_core):
+def basis_pieces_of_pair(bases, first):
     rows = bases.shape[0] // 8 * ZL
     piece = lax.dynamic_slice_in_dim(
         bases, first, rows, 0, allow_negative_indices=False
     )
-    other = lax.ppermute(piece, "core", [(0, 1), (1, 0)])
-    return jnp.where(own_core, piece, other)
+    return piece, lax.ppermute(piece, "core", [(0, 1), (1, 0)])
 
 
 def from_all_x(block):
@@ -87,12 +86,13 @@
 
 
 def per_device(features, out_grads, bases, moment_one, moment_two):
-    projected_low, block = project(features, bases)
+    projected_low, pieces = project(features, bases)
     partial_sum = lax.dot_general(
         projected_low, out_grads, (((0,), (0,)), ((), ())), preferred_element_type=F32
     ).astype(BF16)
-    partial_sum, block = lax.optimization_barrier((partial_sum, block))
-    basis_rows = from_all_x(block)
+    partial_sum, pieces = lax.optimization_barrier((partial_sum, pieces))
+    piece, other, own_core = pieces
+    basis_rows = from_all_x(jnp.where(own_core, piece, other))
     rank, columns = partial_sum.shape
     own = rank // (Y * ZH * ZL)
     blocks = partial_sum.reshape(Y, ZH, ZL, own, columns).transpose(0, 2, 1, 3, 4)

time: 135 us -> 136 us (level)
  the two profiles are of different devices: /device:TPU:8 before, /device:TPU:64 now
where the time goes in v5:
time: 136 us; the launch traced here: 135 us
  blocking collectives  96 us (71%)
  starting transfers between devices  18.3 us (13%)
  waiting for transfers between devices  11.8 us (9%)
  local copies, waits for them, and re-layouts  2.93 us (2%)
  matrix products  2.84 us (2%)
  Pallas kernels  1.79 us (1%)
    all_to_all x4, blocking collectives, exchange(): return lax.all_to_all(blocks, axes, 0, 0)  82.9 us
    all_gather x1, blocking collectives, project(): return (lax.all_gather(my_tokens, TENSOR, axis=0, tiled=True), pieces)  13.2 us
    ppermute x3, waiting for transfers between devices, from_all_x(): blocks.append(lax.ppermute(block, 'x', pairs))  10.3 us
    ppermute x3, starting transfers between devices, from_all_x(): blocks.append(lax.ppermute(block, 'x', pairs))  8.61 us
    all_to_all x1, starting transfers between devices, exchange(): return lax.all_to_all(blocks, axes, 0, 0)  5.84 us
  transfers between devices with their start and end apart: 6, of which 4 were waited for; matrix products, arithmetic and copies ran while one was open for 2% of the time, Pallas kernels for 0%

profile of v5, /device:TPU:64, one launch (start us, length us, event | category | flops | bytes accessed | tf_op | source)
XLA Modules:
  0.0 135.1 jit_solution(9139799327924579339)
XLA Ops:
  0.6 0.0 copy-start
  0.6 0.0 copy-start.1
  0.7 1.5 %constant_dynamic-slice_fusion.1 = (bf16[4,1,72,1024]{3,2,1,0:T(8,128)(2,1)S(1)}, bf16[4,1,72,1024]{3,2,1,0:T(8,128)(2,1)S(1)}) fusion(bf16[4,2,72,1024]{3,2,1,0:T(8,128)(2,1)} %bitcast.45, s32[]{:T(128)S(6)} %select_n.58, s32[]{:T(128)S(6)} %select_n.57), kind=kLoop, calls=%fused_computation.19 | loop fusion | bytes 2359304 | tf_op jit(solution)/shard_map/jit(dynamic_index_in_dim)/dynamic_slice | solution.py:31
  2.2 0.2 copy-done.1
  2.3 0.5 fusion.11
  2.8 1.9 %collective-permute-start = (f32[288,512]{1,0:T(8,128)S(1)}, f32[288,512]{1,0:T(8,128)S(1)}, u32[]{:S(2)}, u32[]{:S(2)}) collective-permute-start(f32[288,512]{1,0:T(8,128)S(1)} %fusion.11), channel_id=1, source_target_pairs={{0,1},{1,0},{2,3},{3,2},{4,5},{5,4},{6,7},{7,6},{8,9},{9,8},{10,11... | collective-permute-start | bytes 1769480 | tf_op jit(solution)/shard_map/ppermute | solution.py:34
  4.7 0.5 fusion.10
  5.2 1.5 %collective-permute-done = f32[288,512]{1,0:T(8,128)S(1)} collective-permute-done((f32[288,512]{1,0:T(8,128)S(1)}, f32[288,512]{1,0:T(8,128)S(1)}, u32[]{:S(2)}, u32[]{:S(2)}) %collective-permute-start) | collective-permute-done | bytes 589856 | tf_op jit(solution)/shard_map/ppermute | solution.py:34
  6.7 0.1 add.47
  6.8 14.6 %all_to_all.25 = f32[4,72,512]{2,1,0:T(8,128)S(1)} all-to-all(f32[4,72,512]{2,1,0:T(8,128)S(1)} %bitcast.39), channel_id=1, replica_groups=mesh['y'=4,'zh'=8,'zl'=2,'x'=4,'core'=2] {'x'}, dimensions={0} | all-to-all | bytes 1179648 | tf_op jit(solution)/shard_map/all_to_all | solution.py:18
  21.4 0.1 constant_dynamic-slice_fusion
  21.5 1.9 %collective-permute-start.1 = (bf16[256,512]{1,0:T(8,128)(2,1)S(1)}, bf16[256,512]{1,0:T(8,128)(2,1)}, u32[]{:S(2)}, u32[]{:S(2)}) collective-permute-start(bf16[256,512]{1,0:T(8,128)(2,1)S(1)} %constant_dynamic-slice_fusion), channel_id=1, source_target_pairs={{0,1},{1,0},{2,3},{3,2},{4,5},{5,4},{6,7},{7,6},{8,9},{9,8},{10,11... | collective-permute-start | bytes 786440 | tf_op jit(solution)/shard_map/ppermute | solution.py:54
  23.4 13.2 %all_gather.3 = bf16[576,512]{1,0:T(8,128)(2,1)S(1)} all-gather(bf16[72,512]{1,0:T(8,128)(2,1)S(1)} %reduce_sum.21), channel_id=1, replica_groups=mesh['y'=4,'zh'=8,'zl'=2,'x'=4,'core'=2] {'x','core'}, dimensions={0}, use_global_device_ids=true | all-gather | bytes 663552 | tf_op jit(solution)/shard_map/all_gather | solution.py:41
  36.6 0.0 copy-done
  36.6 1.4 %convolution_convert_fusion = bf16[512,1408]{1,0:T(8,128)(2,1)S(1)} fusion(bf16[576,512]{1,0:T(8,128)(2,1)S(1)} %all_gather.3, bf16[576,1408]{1,0:T(8,128)(2,1)S(1)} %copy-done), kind=kOutput, calls=%fused_computation | convolution fusion | flops 831193088 | bytes 3653632 | tf_op jit(solution)/shard_map/dot_general | solution.py:90
  38.0 0.0 collective-permute-done.1
  38.1 0.1 copy.9
  38.2 26.2 %all_to_all.26 = bf16[8,64,1408]{2,1,0:T(8,128)(2,1)S(1)} all-to-all(bf16[8,64,1408]{2,1,0:T(8,128)(2,1)S(1)} %bitcast.38), channel_id=1, replica_groups=mesh['y'=4,'zh'=8,'zl'=2,'x'=4,'core'=2] {'y','zl'}, dimensions={0} | all-to-all | bytes 2883584 | tf_op jit(solution)/shard_map/all_to_all | solution.py:18
  64.4 0.2 reduce_sum.22
  64.6 29.1 %all_to_all.27.parts_ref = bf16[8,8,1408]{2,1,0:T(8,128)(2,1)} all-to-all(bf16[8,8,1408]{2,1,0:T(8,128)(2,1)S(1)} %bitcast.47), channel_id=1, replica_groups=mesh['y'=4,'zh'=8,'zl'=2,'x'=4,'core'=2] {'zh'}, dimensions={0} | all-to-all | bytes 360448 | tf_op jit(solution)/shard_map/all_to_all | solution.py:18
  93.7 1.8 %shard_map.76 = (f32[8,1408]{1,0:T(8,128)}, f32[8,1408]{1,0:T(8,128)}, bf16[64,8,176]{2,1,0:T(8,128)(2,1)}) custom-call(bf16[8,8,1408]{2,1,0:T(8,128)(2,1)} %all_to_all.27.parts_ref, f32[8,1408]{1,0:T(8,128)} %one_ref.1, f32[8,1408]{1,0:T(8,128)} %two_ref.1), custom_call_target="tpu_custom_call" | custom-call | tf_op jit(solution)/shard_map/pallas_call | solution.py:105
  95.5 5.8 %all-to-all-start.3 = ((bf16[64,8,176]{2,1,0:T(8,128)(2,1)}), bf16[64,8,176]{2,1,0:T(8,128)(2,1)S(1)}, u32[]{:S(2)}, u32[]{:S(2)}) async-start(bf16[64,8,176]{2,1,0:T(8,128)(2,1)} %get-tuple-element.24), calls=%async_computation.3 | async-start | bytes 524288 | tf_op jit(solution)/shard_map/all_to_all | solution.py:18
  101.4 3.1 %collective-permute-start.4 = (bf16[256,512]{1,0:T(8,128)(2,1)S(1)}, bf16[256,512]{1,0:T(8,128)(2,1)S(1)}, u32[]{:S(2)}, u32[]{:S(2)}) collective-permute-start(bf16[256,512]{1,0:T(8,128)(2,1)S(1)} %broadcast_select_fusion), channel_id=1, source_target_pairs={{0,6},{2,0},{4,2},{6,4},{1,7},{3,1},{5,3},{7,5},{8,14},{10,8},{12,... | collective-permute-start | bytes 786440 | tf_op jit(solution)/shard_map/ppermute | solution.py:62
  104.5 2.8 %collective-permute-start.3 = (bf16[256,512]{1,0:T(8,128)(2,1)S(1)}, bf16[256,512]{1,0:T(8,128)(2,1)S(1)}, u32[]{:S(2)}, u32[]{:S(2)}) collective-permute-start(bf16[256,512]{1,0:T(8,128)(2,1)S(1)} %broadcast_select_fusion), channel_id=1, source_target_pairs={{0,4},{2,6},{4,0},{6,2},{1,5},{3,7},{5,1},{7,3},{8,12},{10,14},{12... | collective-permute-start | bytes 786440 | tf_op jit(solution)/shard_map/ppermute | solution.py:62
  107.2 2.8 %collective-permute-start.2 = (bf16[256,512]{1,0:T(8,128)(2,1)S(1)}, bf16[256,512]{1,0:T(8,128)(2,1)S(1)}, u32[]{:S(2)}, u32[]{:S(2)}) collective-permute-start(bf16[256,512]{1,0:T(8,128)(2,1)S(1)} %broadcast_select_fusion), channel_id=1, source_target_pairs={{0,2},{2,4},{4,6},{6,0},{1,3},{3,5},{5,7},{7,1},{8,10},{10,12},{12... | collective-permute-start | bytes 786440 | tf_op jit(solution)/shard_map/ppermute | solution.py:62
  110.1 2.4 %collective-permute-done.4 = bf16[256,512]{1,0:T(8,128)(2,1)S(1)} collective-permute-done((bf16[256,512]{1,0:T(8,128)(2,1)S(1)}, bf16[256,512]{1,0:T(8,128)(2,1)S(1)}, u32[]{:S(2)}, u32[]{:S(2)}) %collective-permute-start.4) | collective-permute-done | bytes 262176 | tf_op jit(solution)/shard_map/ppermute | solution.py:62
  112.5 4.6 %collective-permute-done.3 = bf16[256,512]{1,0:T(8,128)(2,1)S(1)} collective-permute-done((bf16[256,512]{1,0:T(8,128)(2,1)S(1)}, bf16[256,512]{1,0:T(8,128)(2,1)S(1)}, u32[]{:S(2)}, u32[]{:S(2)}) %collective-permute-start.3) | collective-permute-done | bytes 262176 | tf_op jit(solution)/shard_map/ppermute | solution.py:62
  117.1 3.3 %collective-permute-done.2 = bf16[256,512]{1,0:T(8,128)(2,1)S(1)} collective-permute-done((bf16[256,512]{1,0:T(8,128)(2,1)S(1)}, bf16[256,512]{1,0:T(8,128)(2,1)S(1)}, u32[]{:S(2)}, u32[]{:S(2)}) %collective-permute-start.2) | collective-permute-done | bytes 262176 | tf_op jit(solution)/shard_map/ppermute | solution.py:62
  120.4 0.1 pad_maximum_fusion
  120.5 0.1 dynamic-slice_bitcast_fusion.3
  120.6 0.0 all-to-all-done.3
  120.6 0.5 fusion
  121.1 0.1 copy.14
  121.2 13.0 %all_to_all.28 = bf16[8,128,176]{1,2,0:T(8,128)(2,1)S(1)} all-to-all(bf16[8,128,176]{1,2,0:T(8,128)(2,1)S(1)} %bitcast.43), channel_id=1, replica_groups=mesh['y'=4,'zh'=8,'zl'=2,'x'=4,'core'=2] {'y','zl'}, dimensions={0} | all-to-all | bytes 720896 | tf_op jit(solution)/shard_map/all_to_all | solution.py:18
  134.2 0.9 copy.11
  (2 shorter events, 0.1 us)
Async XLA Ops:
  0.6 36.0 %copy-start = (bf16[576,1408]{1,0:T(8,128)(2,1)S(1)}, bf16[576,1408]{1,0:T(8,128)(2,1)}, u32[]{:S(2)}) copy-start(bf16[576,1408]{1,0:T(8,128)(2,1)} %param.6) | copy-start | bytes 4866052
  0.6 1.7 %copy-start.1 = (bf16[1024,512]{1,0:T(8,128)(2,1)S(1)}, bf16[1024,512]{1,0:T(8,128)(2,1)}, u32[]{:S(2)}) copy-start(bf16[1024,512]{1,0:T(8,128)(2,1)} %param.7) | copy-start | bytes 3145732
  2.8 3.9 %collective-permute-start = (f32[288,512]{1,0:T(8,128)S(1)}, f32[288,512]{1,0:T(8,128)S(1)}, u32[]{:S(2)}, u32[]{:S(2)}) collective-permute-start(f32[288,512]{1,0:T(8,128)S(1)} %fusion.11), channel_id=1, source_target_pairs={{0,1},{1,0},{2,3},{3,2},{4,5},{5,4},{6,7},{7,6},{8,9},{9,8},{10,11... | collective-permute-start | bytes 1769480 | tf_op jit(solution)/shard_map/ppermute | solution.py:34
  21.5 16.5 %collective-permute-start.1 = (bf16[256,512]{1,0:T(8,128)(2,1)S(1)}, bf16[256,512]{1,0:T(8,128)(2,1)}, u32[]{:S(2)}, u32[]{:S(2)}) collective-permute-start(bf16[256,512]{1,0:T(8,128)(2,1)S(1)} %constant_dynamic-slice_fusion), channel_id=1, source_target_pairs={{0,1},{1,0},{2,3},{3,2},{4,5},{5,4},{6,7},{7,6},{8,9},{9,8},{10,11... | collective-permute-start | bytes 786440 | tf_op jit(solution)/shard_map/ppermute | solution.py:54
  95.5 25.1 %all-to-all-start.3 = ((bf16[64,8,176]{2,1,0:T(8,128)(2,1)}), bf16[64,8,176]{2,1,0:T(8,128)(2,1)S(1)}, u32[]{:S(2)}, u32[]{:S(2)}) async-start(bf16[64,8,176]{2,1,0:T(8,128)(2,1)} %get-tuple-element.24), calls=%async_computation.3 | async-start | bytes 524288 | tf_op jit(solution)/shard_map/all_to_all | solution.py:18
  101.4 11.1 %collective-permute-start.4 = (bf16[256,512]{1,0:T(8,128)(2,1)S(1)}, bf16[256,512]{1,0:T(8,128)(2,1)S(1)}, u32[]{:S(2)}, u32[]{:S(2)}) collective-permute-start(bf16[256,512]{1,0:T(8,128)(2,1)S(1)} %broadcast_select_fusion), channel_id=1, source_target_pairs={{0,6},{2,0},{4,2},{6,4},{1,7},{3,1},{5,3},{7,5},{8,14},{10,8},{12,... | collective-permute-start | bytes 786440 | tf_op jit(solution)/shard_map/ppermute | solution.py:62
  104.5 12.6 %collective-permute-start.3 = (bf16[256,512]{1,0:T(8,128)(2,1)S(1)}, bf16[256,512]{1,0:T(8,128)(2,1)S(1)}, u32[]{:S(2)}, u32[]{:S(2)}) collective-permute-start(bf16[256,512]{1,0:T(8,128)(2,1)S(1)} %broadcast_select_fusion), channel_id=1, source_target_pairs={{0,4},{2,6},{4,0},{6,2},{1,5},{3,7},{5,1},{7,3},{8,12},{10,14},{12... | collective-permute-start | bytes 786440 | tf_op jit(solution)/shard_map/ppermute | solution.py:62
  107.2 13.1 %collective-permute-start.2 = (bf16[256,512]{1,0:T(8,128)(2,1)S(1)}, bf16[256,512]{1,0:T(8,128)(2,1)S(1)}, u32[]{:S(2)}, u32[]{:S(2)}) collective-permute-start(bf16[256,512]{1,0:T(8,128)(2,1)S(1)} %broadcast_select_fusion), channel_id=1, source_target_pairs={{0,2},{2,4},{4,6},{6,0},{1,3},{3,5},{5,7},{7,1},{8,10},{10,12},{12... | collective-permute-start | bytes 786440 | tf_op jit(solution)/shard_map/ppermute | solution.py:62

commit v6 on v3

--- a/solution.py
+++ b/solution.py
@@ -96,8 +96,11 @@
     rank, columns = partial_sum.shape
     own = rank // (Y * ZH * ZL)
     blocks = partial_sum.reshape(Y, ZH, ZL, own, columns).transpose(0, 2, 1, 3, 4)
-    blocks = blocks.reshape(Y * ZL, ZH * own, columns)
+    lanes = 128
+    blocks = blocks.reshape(Y * ZL, ZH, own, columns // lanes, lanes)
+    blocks = blocks.transpose(0, 1, 3, 2, 4).reshape(Y * ZL, -1, lanes)
     near = sum_blocks(exchange(blocks, ("y", "zl"))).astype(BF16)
+    near = near.reshape(ZH, columns // lanes, own, lanes).transpose(0, 2, 1, 3)
     arrived = exchange(near.reshape(ZH, own, columns), "zh")
     parts = Y * ZL
     width = columns // parts

time: 135 us -> 135 us (level)
  no operation moved by 1% of the time
where the time goes in v6:
time: 135 us
  blocking collectives  95.9 us (71%)
  starting transfers between devices  17.9 us (13%)
  waiting for transfers between devices  12 us (9%)
  local copies, waits for them, and re-layouts  2.93 us (2%)
  matrix products  2.83 us (2%)
  Pallas kernels  1.79 us (1%)
    all_to_all x4, blocking collectives, exchange(): return lax.all_to_all(blocks, axes, 0, 0)  82.7 us
    all_gather x1, blocking collectives, project(): return (lax.all_gather(my_tokens, TENSOR, axis=0, tiled=True), block)  13.2 us
    ppermute x3, waiting for transfers between devices, from_all_x(): blocks.append(lax.ppermute(block, 'x', pairs))  9.26 us
    ppermute x3, starting transfers between devices, from_all_x(): blocks.append(lax.ppermute(block, 'x', pairs))  8.61 us
    all_to_all x1, starting transfers between devices, exchange(): return lax.all_to_all(blocks, axes, 0, 0)  5.44 us
  transfers between devices with their start and end apart: 6, of which 5 were waited for; matrix products, arithmetic and copies ran while one was open for 2% of the time, Pallas kernels for 0%

profile of v6, /device:TPU:8, one launch (start us, length us, event | category | flops | bytes accessed | tf_op | source)
XLA Modules:
  0.0 134.9 jit_solution(1284313322818306699)
XLA Ops:
  0.6 0.0 copy-start
  0.6 0.0 copy-start.1
  0.7 1.5 %constant_dynamic-slice_fusion.1 = (bf16[4,1,72,1024]{3,2,1,0:T(8,128)(2,1)S(1)}, bf16[4,1,72,1024]{3,2,1,0:T(8,128)(2,1)S(1)}) fusion(bf16[4,2,72,1024]{3,2,1,0:T(8,128)(2,1)} %bitcast.53, s32[]{:T(128)S(6)} %select_n.58, s32[]{:T(128)S(6)} %select_n.57), kind=kLoop, calls=%fused_computation.19 | loop fusion | bytes 2359304 | tf_op jit(solution)/shard_map/jit(dynamic_index_in_dim)/dynamic_slice | solution.py:31
  2.2 0.2 copy-done.1
  2.3 0.5 fusion.11
  2.8 1.9 %collective-permute-start = (f32[288,512]{1,0:T(8,128)S(1)}, f32[288,512]{1,0:T(8,128)S(1)}, u32[]{:S(2)}, u32[]{:S(2)}) collective-permute-start(f32[288,512]{1,0:T(8,128)S(1)} %fusion.11), channel_id=1, source_target_pairs={{0,1},{1,0},{2,3},{3,2},{4,5},{5,4},{6,7},{7,6},{8,9},{9,8},{10,11... | collective-permute-start | bytes 1769480 | tf_op jit(solution)/shard_map/ppermute | solution.py:34
  4.7 0.5 fusion.10
  5.2 1.5 %collective-permute-done = f32[288,512]{1,0:T(8,128)S(1)} collective-permute-done((f32[288,512]{1,0:T(8,128)S(1)}, f32[288,512]{1,0:T(8,128)S(1)}, u32[]{:S(2)}, u32[]{:S(2)}) %collective-permute-start) | collective-permute-done | bytes 589856 | tf_op jit(solution)/shard_map/ppermute | solution.py:34
  6.7 0.1 add.47
  6.8 14.6 %all_to_all.25 = f32[4,72,512]{2,1,0:T(8,128)S(1)} all-to-all(f32[4,72,512]{2,1,0:T(8,128)S(1)} %bitcast.47), channel_id=1, replica_groups=mesh['y'=4,'zh'=8,'zl'=2,'x'=4,'core'=2] {'x'}, dimensions={0} | all-to-all | bytes 1179648 | tf_op jit(solution)/shard_map/all_to_all | solution.py:18
  21.4 0.1 constant_dynamic-slice_fusion
  21.5 1.9 %collective-permute-start.1 = (bf16[256,512]{1,0:T(8,128)(2,1)S(1)}, bf16[256,512]{1,0:T(8,128)(2,1)S(1)}, u32[]{:S(2)}, u32[]{:S(2)}) collective-permute-start(bf16[256,512]{1,0:T(8,128)(2,1)S(1)} %constant_dynamic-slice_fusion), channel_id=1, source_target_pairs={{0,1},{1,0},{2,3},{3,2},{4,5},{5,4},{6,7},{7,6},{8,9},{9,8},{10,11... | collective-permute-start | bytes 786440 | tf_op jit(solution)/shard_map/ppermute | solution.py:54
  23.4 13.2 %all_gather.3 = bf16[576,512]{1,0:T(8,128)(2,1)S(1)} all-gather(bf16[72,512]{1,0:T(8,128)(2,1)S(1)} %reduce_sum.21), channel_id=1, replica_groups=mesh['y'=4,'zh'=8,'zl'=2,'x'=4,'core'=2] {'x','core'}, dimensions={0}, use_global_device_ids=true | all-gather | bytes 663552 | tf_op jit(solution)/shard_map/all_gather | solution.py:41
  36.6 0.0 copy-done
  36.6 1.4 %convolution_convert_fusion = bf16[512,1408]{1,0:T(8,128)(2,1)S(1)} fusion(bf16[576,512]{1,0:T(8,128)(2,1)S(1)} %all_gather.3, bf16[576,1408]{1,0:T(8,128)(2,1)S(1)} %copy-done), kind=kOutput, calls=%fused_computation | convolution fusion | flops 831193088 | bytes 3653632 | tf_op jit(solution)/shard_map/dot_general | solution.py:91
  38.0 0.0 collective-permute-done.1
  38.1 0.1 broadcast_select_fusion
  38.2 0.1 copy.9
  38.3 26.0 %all_to_all.26 = bf16[8,704,128]{2,1,0:T(8,128)(2,1)S(1)} all-to-all(bf16[8,704,128]{2,1,0:T(8,128)(2,1)S(1)} %bitcast.46), channel_id=1, replica_groups=mesh['y'=4,'zh'=8,'zl'=2,'x'=4,'core'=2] {'y','zl'}, dimensions={0} | all-to-all | bytes 2883584 | tf_op jit(solution)/shard_map/all_to_all | solution.py:18
  64.3 0.2 reduce_sum.22
  64.5 30.6 %all_to_all.27.parts_ref = bf16[8,8,1408]{2,1,0:T(8,128)(2,1)} all-to-all(bf16[8,8,1408]{2,1,0:T(8,128)(2,1)S(1)} %bitcast.55), channel_id=1, replica_groups=mesh['y'=4,'zh'=8,'zl'=2,'x'=4,'core'=2] {'zh'}, dimensions={0} | all-to-all | bytes 360448 | tf_op jit(solution)/shard_map/all_to_all | solution.py:18
  95.1 1.8 %shard_map.76 = (f32[8,1408]{1,0:T(8,128)}, f32[8,1408]{1,0:T(8,128)}, bf16[64,8,176]{2,1,0:T(8,128)(2,1)}) custom-call(bf16[8,8,1408]{2,1,0:T(8,128)(2,1)} %all_to_all.27.parts_ref, f32[8,1408]{1,0:T(8,128)} %one_ref.1, f32[8,1408]{1,0:T(8,128)} %two_ref.1), custom_call_target="tpu_custom_call" | custom-call | tf_op jit(solution)/shard_map/pallas_call | solution.py:108
  96.9 5.4 %all-to-all-start.3 = ((bf16[64,8,176]{2,1,0:T(8,128)(2,1)}), bf16[64,8,176]{2,1,0:T(8,128)(2,1)S(1)}, u32[]{:S(2)}, u32[]{:S(2)}) async-start(bf16[64,8,176]{2,1,0:T(8,128)(2,1)} %get-tuple-element.20), calls=%async_computation.3 | async-start | bytes 524288 | tf_op jit(solution)/shard_map/all_to_all | solution.py:18
  102.4 3.1 %collective-permute-start.4 = (bf16[256,512]{1,0:T(8,128)(2,1)S(1)}, bf16[256,512]{1,0:T(8,128)(2,1)S(1)}, u32[]{:S(2)}, u32[]{:S(2)}) collective-permute-start(bf16[256,512]{1,0:T(8,128)(2,1)S(1)} %broadcast_select_fusion), channel_id=1, source_target_pairs={{0,6},{2,0},{4,2},{6,4},{1,7},{3,1},{5,3},{7,5},{8,14},{10,8},{12,... | collective-permute-start | bytes 786440 | tf_op jit(solution)/shard_map/ppermute | solution.py:63
  105.4 2.8 %collective-permute-start.3 = (bf16[256,512]{1,0:T(8,128)(2,1)S(1)}, bf16[256,512]{1,0:T(8,128)(2,1)S(1)}, u32[]{:S(2)}, u32[]{:S(2)}) collective-permute-start(bf16[256,512]{1,0:T(8,128)(2,1)S(1)} %broadcast_select_fusion), channel_id=1, source_target_pairs={{0,4},{2,6},{4,0},{6,2},{1,5},{3,7},{5,1},{7,3},{8,12},{10,14},{12... | collective-permute-start | bytes 786440 | tf_op jit(solution)/shard_map/ppermute | solution.py:63
  108.2 2.8 %collective-permute-start.2 = (bf16[256,512]{1,0:T(8,128)(2,1)S(1)}, bf16[256,512]{1,0:T(8,128)(2,1)S(1)}, u32[]{:S(2)}, u32[]{:S(2)}) collective-permute-start(bf16[256,512]{1,0:T(8,128)(2,1)S(1)} %broadcast_select_fusion), channel_id=1, source_target_pairs={{0,2},{2,4},{4,6},{6,0},{1,3},{3,5},{5,7},{7,1},{8,10},{10,12},{12... | collective-permute-start | bytes 786440 | tf_op jit(solution)/shard_map/ppermute | solution.py:63
  111.1 2.1 %collective-permute-done.4 = bf16[256,512]{1,0:T(8,128)(2,1)S(1)} collective-permute-done((bf16[256,512]{1,0:T(8,128)(2,1)S(1)}, bf16[256,512]{1,0:T(8,128)(2,1)S(1)}, u32[]{:S(2)}, u32[]{:S(2)}) %collective-permute-start.4) | collective-permute-done | bytes 262176 | tf_op jit(solution)/shard_map/ppermute | solution.py:63
  113.2 4.6 %collective-permute-done.3 = bf16[256,512]{1,0:T(8,128)(2,1)S(1)} collective-permute-done((bf16[256,512]{1,0:T(8,128)(2,1)S(1)}, bf16[256,512]{1,0:T(8,128)(2,1)S(1)}, u32[]{:S(2)}, u32[]{:S(2)}) %collective-permute-start.3) | collective-permute-done | bytes 262176 | tf_op jit(solution)/shard_map/ppermute | solution.py:63
  117.9 2.5 %collective-permute-done.2 = bf16[256,512]{1,0:T(8,128)(2,1)S(1)} collective-permute-done((bf16[256,512]{1,0:T(8,128)(2,1)S(1)}, bf16[256,512]{1,0:T(8,128)(2,1)S(1)}, u32[]{:S(2)}, u32[]{:S(2)}) %collective-permute-start.2) | collective-permute-done | bytes 262176 | tf_op jit(solution)/shard_map/ppermute | solution.py:63
  120.3 0.1 pad_maximum_fusion
  120.5 0.1 dynamic-slice_bitcast_fusion.3
  120.6 1.3 all-to-all-done.3
  121.8 0.5 fusion
  122.3 0.1 copy.14
  122.4 11.5 %all_to_all.28 = bf16[8,128,176]{1,2,0:T(8,128)(2,1)S(1)} all-to-all(bf16[8,128,176]{1,2,0:T(8,128)(2,1)S(1)} %bitcast.51), channel_id=1, replica_groups=mesh['y'=4,'zh'=8,'zl'=2,'x'=4,'core'=2] {'y','zl'}, dimensions={0} | all-to-all | bytes 720896 | tf_op jit(solution)/shard_map/all_to_all | solution.py:18
  133.9 0.9 copy.11
  (1 shorter events, 0.0 us)
Async XLA Ops:
  0.6 36.0 %copy-start = (bf16[576,1408]{1,0:T(8,128)(2,1)S(1)}, bf16[576,1408]{1,0:T(8,128)(2,1)}, u32[]{:S(2)}) copy-start(bf16[576,1408]{1,0:T(8,128)(2,1)} %param.6) | copy-start | bytes 4866052
  0.6 1.7 %copy-start.1 = (bf16[1024,512]{1,0:T(8,128)(2,1)S(1)}, bf16[1024,512]{1,0:T(8,128)(2,1)}, u32[]{:S(2)}) copy-start(bf16[1024,512]{1,0:T(8,128)(2,1)} %param.7) | copy-start | bytes 3145732
  2.8 3.9 %collective-permute-start = (f32[288,512]{1,0:T(8,128)S(1)}, f32[288,512]{1,0:T(8,128)S(1)}, u32[]{:S(2)}, u32[]{:S(2)}) collective-permute-start(f32[288,512]{1,0:T(8,128)S(1)} %fusion.11), channel_id=1, source_target_pairs={{0,1},{1,0},{2,3},{3,2},{4,5},{5,4},{6,7},{7,6},{8,9},{9,8},{10,11... | collective-permute-start | bytes 1769480 | tf_op jit(solution)/shard_map/ppermute | solution.py:34
  21.5 16.5 %collective-permute-start.1 = (bf16[256,512]{1,0:T(8,128)(2,1)S(1)}, bf16[256,512]{1,0:T(8,128)(2,1)S(1)}, u32[]{:S(2)}, u32[]{:S(2)}) collective-permute-start(bf16[256,512]{1,0:T(8,128)(2,1)S(1)} %constant_dynamic-slice_fusion), channel_id=1, source_target_pairs={{0,1},{1,0},{2,3},{3,2},{4,5},{5,4},{6,7},{7,6},{8,9},{9,8},{10,11... | collective-permute-start | bytes 786440 | tf_op jit(solution)/shard_map/ppermute | solution.py:54
  96.9 24.9 %all-to-all-start.3 = ((bf16[64,8,176]{2,1,0:T(8,128)(2,1)}), bf16[64,8,176]{2,1,0:T(8,128)(2,1)S(1)}, u32[]{:S(2)}, u32[]{:S(2)}) async-start(bf16[64,8,176]{2,1,0:T(8,128)(2,1)} %get-tuple-element.20), calls=%async_computation.3 | async-start | bytes 524288 | tf_op jit(solution)/shard_map/all_to_all | solution.py:18
  102.4 10.9 %collective-permute-start.4 = (bf16[256,512]{1,0:T(8,128)(2,1)S(1)}, bf16[256,512]{1,0:T(8,128)(2,1)S(1)}, u32[]{:S(2)}, u32[]{:S(2)}) collective-permute-start(bf16[256,512]{1,0:T(8,128)(2,1)S(1)} %broadcast_select_fusion), channel_id=1, source_target_pairs={{0,6},{2,0},{4,2},{6,4},{1,7},{3,1},{5,3},{7,5},{8,14},{10,8},{12,... | collective-permute-start | bytes 786440 | tf_op jit(solution)/shard_map/ppermute | solution.py:63
  105.4 12.4 %collective-permute-start.3 = (bf16[256,512]{1,0:T(8,128)(2,1)S(1)}, bf16[256,512]{1,0:T(8,128)(2,1)S(1)}, u32[]{:S(2)}, u32[]{:S(2)}) collective-permute-start(bf16[256,512]{1,0:T(8,128)(2,1)S(1)} %broadcast_select_fusion), channel_id=1, source_target_pairs={{0,4},{2,6},{4,0},{6,2},{1,5},{3,7},{5,1},{7,3},{8,12},{10,14},{12... | collective-permute-start | bytes 786440 | tf_op jit(solution)/shard_map/ppermute | solution.py:63
  108.2 12.1 %collective-permute-start.2 = (bf16[256,512]{1,0:T(8,128)(2,1)S(1)}, bf16[256,512]{1,0:T(8,128)(2,1)S(1)}, u32[]{:S(2)}, u32[]{:S(2)}) collective-permute-start(bf16[256,512]{1,0:T(8,128)(2,1)S(1)} %broadcast_select_fusion), channel_id=1, source_target_pairs={{0,2},{2,4},{4,6},{6,0},{1,3},{3,5},{5,7},{7,1},{8,10},{10,12},{12... | collective-permute-start | bytes 786440 | tf_op jit(solution)/shard_map/ppermute | solution.py:63
